TPU v7x, 32 devices: a whole 2x2x4 slice. The times are simulated.
32 devices in a mesh: ep: 16 (over z, y, core), tp: 2 (over x).
Axes of the slice: x: 2, y: 2, z: 4, core: 2. Of those that a mesh axis runs over, the one named last changes fastest.
Arguments:
- tokens: bfloat16 [2048, 2048], P('ep'), may hold values from -6 to 6
- expert_ids: int32 [2048, 8], P('ep'), may hold values from 0 to 31, all different within a row; in each aligned block of 128 rows (0 to 127, 128 to 255, ...) at most 48 rows name the same one
- combine: float32 [2048, 8], P('ep'), may hold values from 0.05 to 0.5
- cotangent: bfloat16 [2048, 2048], P('ep'), may hold values from -6 to 6
- old_layout: int32 [32], replicated, may hold values from 0 to 31, each once
- pair_moves: int32 [16], replicated, may hold values from 0 to 1, as said below
- gate_w: bfloat16 [32, 2048, 768], P('ep', None, 'tp'), may hold values from -0.125 to 0.125
- up_w: bfloat16 [32, 2048, 768], P('ep', None, 'tp'), may hold values from -0.125 to 0.125
- down_w: bfloat16 [32, 768, 2048], P('ep', 'tp'), may hold values from -0.21875 to 0.21875
Outputs:
- mixed: bfloat16 [2048, 2048], P('ep', 'tp')
- d_tokens: bfloat16 [2048, 2048], P('ep', 'tp')
- d_combine: float32 [2048, 8], P('ep')
- grad_gate: bfloat16 [32, 2048, 768], P('ep', None, 'tp')
- grad_up: bfloat16 [32, 2048, 768], P('ep', None, 'tp')
- grad_down: bfloat16 [32, 768, 2048], P('ep', 'tp')
Inputs may be any that keep to these rules, and one draw needn't show every extreme that they name: `expert_ids`: among the 128 tokens of one ep index no expert is named more than 48 times, a bound that some block reaches. `old_layout`: A permutation of the experts. pair_moves[q] = pair_moves[q + 8]; at least one pair moves.
All inputs are finite; a program needn't handle non-finite values.
Results may differ from a plain program's by a relative error of at most 0.008.
Values may be sent and summed in bfloat16 or wider, within the bound.
No kernel may reach another device: no remote copies, remote signals or barrier semaphores. Data moves between devices by JAX's collectives and lax.ppermute only.
A program may use at most 192 MiB of HBM per device.

v0:
```python
import jax
import jax.numpy as jnp
from jax import lax
from jax.sharding import PartitionSpec as P


def from_partner(value, axis, distance):
    mask = 2**distance
    pairs = [(source, source ^ mask) for source in range(lax.axis_size(axis))]
    return lax.ppermute(value, axis, pairs)


def body(tokens, expert_ids, combine, cotangent, old_layout, pair_moves, gate_w, up_w, down_w):
    ep_count = lax.axis_size("ep")
    tp_count = lax.axis_size("tp")
    tok_count, top_k = expert_ids.shape
    expert_count = old_layout.shape[0]
    per_device = gate_w.shape[0]
    model_width = tokens.shape[1]
    share_width = model_width // tp_count
    capacity = 3 * tok_count * top_k // (2 * expert_count)
    pair_count = ep_count // 2
    swap_bit = ep_count.bit_length() - 2
    my_index = lax.axis_index("ep")
    my_share = lax.axis_index("tp")
    my_move = pair_moves[my_index] == 1
    slot_ids = jnp.arange(expert_count, dtype=jnp.int32)
    slot_device = slot_ids // per_device
    slot_local = slot_ids % per_device
    moved = (slot_local == per_device - 1) & (pair_moves[slot_device] == 1)
    source_slot = jnp.where(
        moved, (slot_device + pair_count) % ep_count * per_device + slot_local, slot_ids
    )
    new_layout = jnp.sum(
        jnp.where(source_slot[:, None] == slot_ids[None, :], old_layout[None, :], 0), axis=1
    )
    w_gate, w_up, w_down = (gate_w, up_w, down_w)
    arrived = from_partner(
        (gate_w[per_device - 1], up_w[per_device - 1], down_w[per_device - 1]), "ep", swap_bit
    )
    w_gate = jnp.concatenate(
        [gate_w[:-1], jnp.where(my_move, arrived[0], gate_w[-1])[None]], axis=0
    )
    w_up = jnp.concatenate([up_w[:-1], jnp.where(my_move, arrived[1], up_w[-1])[None]], axis=0)
    w_down = jnp.concatenate(
        [down_w[:-1], jnp.where(my_move, arrived[2], down_w[-1])[None]], axis=0
    )
    slot_of = jnp.sum(
        jnp.where(new_layout[None, :] == slot_ids[:, None], slot_ids[None, :], 0), axis=1
    )
    flat_ids = expert_ids.reshape(-1)
    onehot = (flat_ids[:, None] == slot_ids[None, :]).astype(jnp.int32)
    before = jnp.cumsum(onehot, axis=0) - onehot
    position = jnp.sum(before * onehot, axis=1)
    target_slot = jnp.sum(onehot * slot_of[None, :], axis=1)
    target_device = target_slot // per_device
    target_local = target_slot % per_device
    row_index = target_local * (ep_count * capacity) + target_device * capacity + position
    rows_total = expert_count * capacity
    matches = jnp.arange(rows_total, dtype=jnp.int32)[:, None] == row_index[None, :]
    select = jnp.sum(
        matches.reshape(rows_total, tok_count, top_k).astype(jnp.int32), axis=2
    ).astype(jnp.bfloat16)
    row_weight = jnp.sum(jnp.where(matches, combine.reshape(-1)[None, :], 0.0), axis=1)

    def dispatch(source, scaling):
        portion = lax.dynamic_slice_in_dim(source, my_share * share_width, share_width, 1)
        picked = jnp.dot(select, portion, preferred_element_type=jnp.float32)
        if scaling is not None:
            picked = picked * scaling[:, None]
        buffer = picked.astype(jnp.bfloat16).reshape(per_device, ep_count * capacity, share_width)
        landed = lax.all_to_all(buffer, "ep", split_axis=1, concat_axis=1, tiled=True)
        return lax.all_gather(landed, "tp", axis=2, tiled=True)

    def send_back(partial_value):
        shares = lax.psum_scatter(partial_value, "tp", scatter_dimension=2, tiled=True).astype(
            jnp.bfloat16
        )
        returned = lax.all_to_all(shares, "ep", split_axis=1, concat_axis=1, tiled=True)
        return returned.reshape(rows_total, share_width)[row_index].reshape(
            tok_count, top_k, share_width
        )

    rows_in = dispatch(tokens, None)
    gate = jnp.einsum("erd,edf->erf", rows_in, w_gate, preferred_element_type=jnp.float32)
    upper = jnp.einsum("erd,edf->erf", rows_in, w_up, preferred_element_type=jnp.float32)
    sigma = jax.nn.sigmoid(gate)
    active = gate * sigma
    hidden = (active * upper).astype(jnp.bfloat16)
    out_part = jnp.einsum("erf,efd->erd", hidden, w_down, preferred_element_type=jnp.float32)
    out_rows = send_back(out_part).astype(jnp.float32)
    mixed = jnp.einsum("tk,tkd->td", combine, out_rows).astype(jnp.bfloat16)
    cot_share = lax.dynamic_slice_in_dim(cotangent, my_share * share_width, share_width, 1).astype(
        jnp.float32
    )
    combine_part = jnp.einsum("td,tkd->tk", cot_share, out_rows)
    d_combine = lax.psum(combine_part, "tp")
    rows_grad = dispatch(cotangent, row_weight)
    d_hidden = jnp.einsum("erd,efd->erf", rows_grad, w_down, preferred_element_type=jnp.float32)
    d_gate = (d_hidden * upper * sigma * (1.0 + gate * (1.0 - sigma))).astype(jnp.bfloat16)
    d_up = (d_hidden * active).astype(jnp.bfloat16)
    back_part = jnp.einsum(
        "erf,edf->erd", d_gate, w_gate, preferred_element_type=jnp.float32
    ) + jnp.einsum("erf,edf->erd", d_up, w_up, preferred_element_type=jnp.float32)
    back_rows = send_back(back_part)
    d_tokens = jnp.sum(back_rows.astype(jnp.float32), axis=1).astype(jnp.bfloat16)
    grad_gate = jnp.einsum(
        "erd,erf->edf", rows_in, d_gate, preferred_element_type=jnp.float32
    ).astype(jnp.bfloat16)
    grad_up = jnp.einsum("erd,erf->edf", rows_in, d_up, preferred_element_type=jnp.float32).astype(
        jnp.bfloat16
    )
    grad_down = jnp.einsum(
        "erf,erd->efd", hidden, rows_grad, preferred_element_type=jnp.float32
    ).astype(jnp.bfloat16)
    return (mixed, d_tokens, d_combine, grad_gate, grad_up, grad_down)


def solution(mesh):
    return jax.shard_map(
        body,
        mesh=mesh,
        in_specs=(
            P("ep", None),
            P("ep", None),
            P("ep", None),
            P("ep", None),
            P(),
            P(),
            P("ep", None, "tp"),
            P("ep", None, "tp"),
            P("ep", "tp", None),
        ),
        out_specs=(
            P("ep", "tp"),
            P("ep", "tp"),
            P("ep", None),
            P("ep", None, "tp"),
            P("ep", None, "tp"),
            P("ep", "tp", None),
        ),
        check_vma=False,
    )
```

profile of v0, /device:TPU:16, one launch (start us, length us, event | category | flops | bytes accessed | tf_op | source)
XLA Modules:
  0.0 845.0 jit_solution(14290538702906426024)
XLA Ops:
  10.6 9.0 %reduce-window.6 = s32[32,8,128]{2,1,0:T(8,128)S(1)} reduce-window(s32[32,8,128]{2,1,0:T(8,128)S(1)} %fusion.18, s32[]{:T(128)} %constant.84.clone.1), window={size=1x1x128 pad=0_0x0_0x127_0}, to_apply=%region_3.4 | reduce-window | flops 4161536 | bytes 262148 | tf_op jit(solution)/shard_map/reduce-window
  20.5 8.0 convert_reduce_fusion
  29.5 4.9 copy.68
  34.4 6.3 all-to-all-start
  41.0 70.0 %all-to-all-done = bf16[2,768,1024]{2,0,1:T(2,128)(2,1)} async-done(((bf16[2,768,1024]{2,0,1:T(2,128)(2,1)}), bf16[2,768,1024]{2,0,1:T(2,128)(2,1)}, u32[]{:S(2)}, u32[]{:S(2)}) %all-to-all-start) | async-done | bytes 3145760 | tf_op jit(solution)/shard_map/all_to_all | solution.py:72
  111.0 4.5 copy.69
  120.7 74.6 %all_to_all.20 = bf16[2,768,1024]{2,0,1:T(2,128)(2,1)S(1)} all-to-all(bf16[2,768,1024]{2,0,1:T(2,128)(2,1)S(1)} %copy.73), channel_id=1, replica_groups=mesh['ep'=16,'tp'=2] {'ep'}, dimensions={1} | all-to-all | bytes 6291456 | tf_op jit(solution)/shard_map/all_to_all | solution.py:72
  198.0 4.0 fusion.52
  210.2 127.9 %collective-permute-done = bf16[2048,384]{1,0:T(8,128)(2,1)S(1)} collective-permute-done((bf16[2048,384]{1,0:T(8,128)(2,1)}, bf16[2048,384]{1,0:T(8,128)(2,1)S(1)}, u32[]{:S(2)}, u32[]{:S(2)}) %collective-permute-start) | collective-permute-done | bytes 1572896 | tf_op jit(solution)/shard_map/ppermute | solution.py:10
  341.5 30.3 %collective-permute-done.1 = bf16[2048,384]{1,0:T(8,128)(2,1)} collective-permute-done((bf16[2048,384]{1,0:T(8,128)(2,1)}, bf16[2048,384]{1,0:T(8,128)(2,1)}, u32[]{:S(2)}, u32[]{:S(2)}) %collective-permute-start.1) | collective-permute-done | bytes 1572896 | tf_op jit(solution)/shard_map/ppermute | solution.py:10
  374.6 30.6 %collective-permute-done.2 = bf16[384,2048]{1,0:T(8,128)(2,1)} collective-permute-done((bf16[384,2048]{1,0:T(8,128)(2,1)}, bf16[384,2048]{1,0:T(8,128)(2,1)}, u32[]{:S(2)}, u32[]{:S(2)}) %collective-permute-start.2) | collective-permute-done | bytes 1572896 | tf_op jit(solution)/shard_map/ppermute | solution.py:10
  408.0 8.5 %fusion.8 = f32[2,768,384]{2,1,0:T(8,128)} fusion(bf16[2,768,2048]{2,1,0:T(8,128)(2,1)} %all-gather.3.cloned.1.call-done, bf16[1,2048,384]{2,1,0:T(8,128)(2,1)} %select_bitcast_fusion.1, bf16[1,2048,384]{2,1,0:T(8,128)(2,1)} %get-tuple-element.15), kind=kOutput, calls=%fused_computation.29 | convolution fusion | flops 2417491968 | bytes 11796480 | tf_op jit(solution)/shard_map/erd,edf->erf/dot_general | solution.py:86
  416.5 6.8 fusion.5
  423.4 5.8 multiply_convert_fusion.2
  429.2 3.5 fusion.7
  432.7 7.7 convolution_add_fusion
  441.8 10.4 %fusion.6 = f32[2,768,2048]{2,1,0:T(8,128)} fusion(bf16[2,768,384]{2,1,0:T(8,128)(2,1)} %get-tuple-element.10, bf16[1,384,2048]{2,1,0:T(8,128)(2,1)S(1)} %copy-done.7, bf16[1,384,2048]{2,1,0:T(8,128)(2,1)} %get-tuple-element.11), kind=kOutput, calls=%fused_computation.27 | convolution fusion | flops 2417491968 | bytes 16908288 | tf_op jit(solution)/shard_map/erf,efd->erd/dot_general | solution.py:90
  452.2 134.5 %reduce-scatter.5.cloned.1.call-done = f32[2,768,1024]{2,1,0:T(8,128)} async-done(((f32[2,768,2048]{2,1,0:T(8,128)}), f32[2,768,1024]{2,1,0:T(8,128)}) %reduce-scatter.5.cloned.1.call-update) | async-done | bytes 6291472 | tf_op jit(solution)/shard_map/reduce_scatter | solution.py:76
  590.0 4.9 copy.75
  594.9 6.0 all-to-all-start.3
  600.9 132.4 %reduce-scatter.3.cloned.1.call-done = f32[2,768,1024]{2,1,0:T(8,128)} async-done(((f32[2,768,2048]{2,1,0:T(8,128)}), f32[2,768,1024]{2,1,0:T(8,128)}) %reduce-scatter.3.cloned.1.call-update) | async-done | bytes 6291472 | tf_op jit(solution)/shard_map/reduce_scatter | solution.py:76
  736.6 4.9 copy.70
  741.5 6.5 all-to-all-start.1
  749.0 7.3 convolution_convert_fusion.1
  756.2 8.1 convolution_convert_fusion.3
  764.3 4.9 convolution_convert_fusion.2
  769.2 4.6 copy.76
  773.8 7.5 gather_fusion.2
  783.4 34.7 %all-to-all-done.1 = bf16[2,768,1024]{2,0,1:T(2,128)(2,1)} async-done(((bf16[2,768,1024]{2,0,1:T(2,128)(2,1)}), bf16[2,768,1024]{2,0,1:T(2,128)(2,1)}, u32[]{:S(2)}, u32[]{:S(2)}) %all-to-all-start.1) | async-done | bytes 3145760 | tf_op jit(solution)/shard_map/all_to_all | solution.py:79
  818.1 4.5 copy.71
  822.6 7.3 gather_fusion.1
  832.7 5.5 psum.7
  (102 shorter events, 43.6 us)
Async XLA Ops:
  7.2 109.3 %copy-start = (bf16[128,2048]{1,0:T(8,128)(2,1)S(1)}, bf16[128,2048]{1,0:T(8,128)(2,1)}, u32[]{:S(2)}) copy-start(bf16[128,2048]{1,0:T(8,128)(2,1)} %param.12) | copy-start | bytes 1572868
  7.2 21.4 %copy-start.14 = (bf16[128,2048]{1,0:T(8,128)(2,1)S(1)}, bf16[128,2048]{1,0:T(8,128)(2,1)}, u32[]{:S(2)}) copy-start(bf16[128,2048]{1,0:T(8,128)(2,1)} %param.9) | copy-start | bytes 1572868
  34.4 6.4 copy-start.15
  34.4 76.5 %all-to-all-start = ((bf16[2,768,1024]{2,0,1:T(2,128)(2,1)}), bf16[2,768,1024]{2,0,1:T(2,128)(2,1)}, u32[]{:S(2)}, u32[]{:S(2)}) async-start(bf16[2,768,1024]{2,0,1:T(2,128)(2,1)} %copy.68), calls=%async_computation | async-start | bytes 6291456 | tf_op jit(solution)/shard_map/all_to_all | solution.py:72
  40.7 367.3 %all-gather.3.cloned.1.call-start = ((), (), s32[]{:S(2)}) async-start(), calls=%async_computation.6 | async-start | bytes 9437184 | tf_op jit(solution)/shard_map/all_gather | solution.py:73
  115.5 301.0 %all-gather.5.cloned.1.call-start = ((), (), s32[]{:S(2)}) async-start(), calls=%async_computation.8 | async-start | bytes 9437184 | tf_op jit(solution)/shard_map/all_gather | solution.py:73
  197.9 388.8 %reduce-scatter.5.cloned.1.call-start = ((), (), s32[]{:S(2)}) async-start(), calls=%async_computation.9 | async-start | bytes 18874368 | tf_op jit(solution)/shard_map/reduce_scatter | solution.py:76
  197.9 4.0 copy-start.2
  202.0 4.9 copy-start.4
  202.0 136.1 %collective-permute-start = (bf16[2048,384]{1,0:T(8,128)(2,1)}, bf16[2048,384]{1,0:T(8,128)(2,1)S(1)}, u32[]{:S(2)}, u32[]{:S(2)}) collective-permute-start(bf16[2048,384]{1,0:T(8,128)(2,1)} %get-tuple-element.14), channel_id=1, source_target_pairs={{0,16},{2,18},{4,20},{6,22},{8,24},{10,26},{12,28},{14,30},{16,0},... | collective-permute-start | bytes 4718600 | tf_op jit(solution)/shard_map/ppermute | solution.py:10
  204.0 5.0 copy-start.1
  204.0 167.8 %collective-permute-start.1 = (bf16[2048,384]{1,0:T(8,128)(2,1)}, bf16[2048,384]{1,0:T(8,128)(2,1)}, u32[]{:S(2)}, u32[]{:S(2)}) collective-permute-start(bf16[2048,384]{1,0:T(8,128)(2,1)} %get-tuple-element.16), channel_id=1, source_target_pairs={{0,16},{2,18},{4,20},{6,22},{8,24},{10,26},{12,28},{14,30},{16,0},... | collective-permute-start | bytes 4718600 | tf_op jit(solution)/shard_map/ppermute | solution.py:10
  209.0 196.2 %collective-permute-start.2 = (bf16[384,2048]{1,0:T(8,128)(2,1)}, bf16[384,2048]{1,0:T(8,128)(2,1)}, u32[]{:S(2)}, u32[]{:S(2)}) collective-permute-start(bf16[384,2048]{1,0:T(8,128)(2,1)} %get-tuple-element.12), channel_id=1, source_target_pairs={{0,16},{2,18},{4,20},{6,22},{8,24},{10,26},{12,28},{14,30},{16,0},... | collective-permute-start | bytes 4718600 | tf_op jit(solution)/shard_map/ppermute | solution.py:10
  338.1 1.2 copy-start.10
  339.3 32.6 %copy-start.3 = (bf16[2,2048,384]{2,1,0:T(8,128)(2,1)S(1)}, bf16[2,2048,384]{2,1,0:T(8,128)(2,1)}, u32[]{:S(2)}) copy-start(bf16[2,2048,384]{2,1,0:T(8,128)(2,1)} %param.16) | copy-start | bytes 9437188
  341.5 63.7 %copy-start.5 = (bf16[2,384,2048]{2,1,0:T(8,128)(2,1)S(1)}, bf16[2,384,2048]{2,1,0:T(8,128)(2,1)}, u32[]{:S(2)}) copy-start(bf16[2,384,2048]{2,1,0:T(8,128)(2,1)} %param.17) | copy-start | bytes 9437188
  416.5 6.9 copy-start.6
  416.5 6.9 copy-start.16
  416.5 6.9 copy-start.17
  423.4 5.8 copy-start.8
  423.4 5.8 copy-start.9
  440.4 1.4 copy-start.7
  440.4 292.9 %reduce-scatter.3.cloned.1.call-start = ((), (), s32[]{:S(2)}) async-start(), calls=%async_computation.7 | async-start | bytes 18874368 | tf_op jit(solution)/shard_map/reduce_scatter | solution.py:76
  594.9 146.7 %all-to-all-start.3 = ((bf16[2,768,1024]{2,0,1:T(2,128)(2,1)}), bf16[2,768,1024]{2,0,1:T(2,128)(2,1)}, u32[]{:S(2)}, u32[]{:S(2)}) async-start(bf16[2,768,1024]{2,0,1:T(2,128)(2,1)} %copy.75), calls=%async_computation.5 | async-start | bytes 6291456 | tf_op jit(solution)/shard_map/all_to_all | solution.py:79
  741.5 7.4 copy-start.12
  741.5 76.6 %all-to-all-start.1 = ((bf16[2,768,1024]{2,0,1:T(2,128)(2,1)}), bf16[2,768,1024]{2,0,1:T(2,128)(2,1)}, u32[]{:S(2)}, u32[]{:S(2)}) async-start(bf16[2,768,1024]{2,0,1:T(2,128)(2,1)} %copy.70), calls=%async_computation.2 | async-start | bytes 6291456 | tf_op jit(solution)/shard_map/all_to_all | solution.py:79
  748.9 7.3 copy-start.11
  748.9 15.4 %slice-start = ((s8[6291456]{0:T(1024)(128)(4,1)}), s8[4194304]{0:T(1024)(128)(4,1)S(1)}, s32[]{:S(2)}) async-start(s8[6291456]{0:T(1024)(128)(4,1)} %bitcast.85), calls=%async_computation.10 | async-start | bytes 8388608
  756.2 8.1 slice-start.1
  829.9 1.2 copy-start.13
Sparse Core Ops, SparseCore 0:
  115.6 79.9 all-gather.2
  198.0 80.1 all-gather.4
  440.5 146.1 reduce-scatter.4
  588.8 144.4 reduce-scatter.2
where the time goes:
time: 853 us; the launch traced here: 845 us
  waiting for transfers between devices  560 us (66%)
  blocking collectives  80.1 us (9%)
  matrix products  66.9 us (8%)
  local copies, waits for them, and re-layouts  64.6 us (8%)
  other arithmetic  35.5 us (4%)
  starting transfers between devices  22.5 us (3%)
  between operations  15 us (2%)
    reduce_scatter x2, waiting for transfers between devices, send_back(): lax.psum_scatter(partial_value, 'tp', scatter_dimension=2, tiled=True)  267 us
    ppermute x3, waiting for transfers between devices, from_partner(): return lax.ppermute(value, axis, pairs)  189 us
    all_to_all x1, blocking collectives, dispatch(): lax.all_to_all(buffer, 'ep', split_axis=1, concat_axis=1, tiled=True)  74.6 us
    all_to_all x1, waiting for transfers between devices, dispatch(): lax.all_to_all(buffer, 'ep', split_axis=1, concat_axis=1, tiled=True)  70 us
    all_to_all x2, waiting for transfers between devices, send_back(): lax.all_to_all(shares, 'ep', split_axis=1, concat_axis=1, tiled=True)  34.7 us
  transfers between devices with their start and end apart: 10, of which 7 were waited for; matrix products, arithmetic and copies ran while one was open for 11% of the time, Pallas kernels for 0%

commit v1 on v0

--- a/solution.py
+++ b/solution.py
@@ -1,16 +1,188 @@
 import jax
 import jax.numpy as jnp
+import numpy as np
 from jax import lax
 from jax.sharding import PartitionSpec as P
 
-
-def from_partner(value, axis, distance):
+F32 = jnp.float32
+BF16 = jnp.bfloat16
+
+
+def ring_order(chips):
+    return list(range(0, chips, 2)) + list(range(chips - 1, 0, -2))
+
+
+def ring_pairs(order, hop):
+    chips = len(order)
+    return [
+        (chip * 2 + core, order[(place + hop) % chips] * 2 + core)
+        for place, chip in enumerate(order)
+        for core in range(2)
+    ]
+
+
+def block_tables(order):
+    chips = len(order)
+    half = chips // 2
+    hops = [0] + [hop for step in range(1, half) for hop in (-step, step)] + [half]
+    ep_count = 2 * chips
+    arrival = np.zeros((ep_count, ep_count), np.int32)
+    for place, chip in enumerate(order):
+        for core in range(2):
+            arrival[chip * 2 + core] = [
+                order[(place + hop) % chips] * 2 + (core ^ side) for hop in hops for side in range(2)
+            ]
+    spot = np.argsort(arrival, axis=1).astype(np.int32)
+    partner = np.arange(ep_count) ^ (ep_count // 2)
+    from_partner = np.take_along_axis(spot[partner], arrival, axis=1).astype(np.int32)
+    return arrival, spot, from_partner
+
+
+def dot(a, b, ca, cb):
+    return lax.dot_general(a, b, (((ca,), (cb,)), ((), ())), preferred_element_type=F32)
+
+
+def gather_body(tokens, expert_ids, combine, cotangent, old_layout, pair_moves, gate_w, up_w, down_w):
+    ep_count = lax.axis_size("ep")
+    tp_count = lax.axis_size("tp")
+    tok_count, top_k = expert_ids.shape
+    expert_count = old_layout.shape[0]
+    per_device, width, units = gate_w.shape
+    share = width // tp_count
+    capacity = 3 * tok_count * top_k // (2 * expert_count)
+    chips = ep_count // 2
+    half = chips // 2
+    order = ring_order(chips)
+    forward, backward = ring_pairs(order, 1), ring_pairs(order, -1)
+    other_core = [(i, i ^ 1) for i in range(ep_count)]
+    other_share = [(i, i ^ 1) for i in range(tp_count)]
+    partners = [(i, i ^ (ep_count // 2)) for i in range(ep_count)]
+    me = lax.axis_index("ep")
+    my_share = lax.axis_index("tp")
+    arrival, spot, from_partner = (jnp.asarray(table)[me] for table in block_tables(order))
+
+    meta = lax.all_gather(
+        jnp.concatenate([expert_ids.astype(F32), combine], axis=1), "ep", axis=0, tiled=False
+    )
+    meta = jnp.take(meta, arrival, axis=0)
+    ids = meta[:, :, :top_k].astype(jnp.int32)
+    weights = meta[:, :, top_k:]
+    my_move = pair_moves[me] == 1
+    last = per_device - 1
+    experts = lax.dynamic_slice_in_dim(old_layout, me * per_device, per_device, 0)
+    partner_last = old_layout[(me ^ (ep_count // 2)) * per_device + last]
+    new_last = jnp.where(my_move, partner_last, experts[last])
+    chosen = ids[:, :, None, :] == experts[None, None, :, None]
+    scale = jnp.sum(jnp.where(chosen, weights[:, :, None, :], 0.0), axis=3)
+    earlier = (jnp.arange(tok_count)[:, None] < jnp.arange(tok_count)[None, :]).astype(BF16)
+
+    def rows_of(expert):
+        named = jnp.any(ids == expert, axis=2)
+        position = jnp.dot(named.astype(BF16), earlier, preferred_element_type=F32).astype(jnp.int32)
+        wanted = jnp.arange(capacity, dtype=jnp.int32)[None, :, None]
+        return ((position[:, None, :] == wanted) & named[:, None, :]).astype(BF16)
+
+    both = per_device * units
+    w_in = jnp.concatenate([gate_w[l] for l in range(per_device)] + [up_w[l] for l in range(per_device)], axis=1)
+    w_out = down_w.reshape(both, width)
+    mine_at, other_at = my_share * share, (1 - my_share) * share
+    w_in_mine = lax.dynamic_slice_in_dim(w_in, mine_at, share, 0)
+    w_in_other = lax.dynamic_slice_in_dim(w_in, other_at, share, 0)
+    w_out_mine = lax.dynamic_slice_in_dim(w_out, mine_at, share, 1)
+    w_out_other = lax.dynamic_slice_in_dim(w_out, other_at, share, 1)
+
+    def group_pass(pieces, first):
+        near = jnp.stack(pieces)
+        far = lax.ppermute(near, "ep", other_core)
+        count = len(pieces)
+        group = jnp.stack([near, far], axis=1).reshape(count * 2 * tok_count, 2 * width)
+        x, cot = group[:, :width], group[:, width:]
+        gains = scale[first : first + 2 * count].reshape(-1, per_device)
+        gains_wide = jnp.repeat(gains, units, axis=1)
+        projected = dot(x, w_in, 1, 0)
+        pulled = dot(cot, w_out, 1, 1)
+        gate, upper = projected[:, :both], projected[:, both:]
+        sigma = jax.nn.sigmoid(gate)
+        active = gate * sigma
+        hidden = active * upper
+        d_combine_part = jnp.sum((hidden * pulled).reshape(-1, per_device, units), axis=2)
+        d_hidden = pulled * gains_wide
+        hidden = (hidden * gains_wide).astype(BF16)
+        d_gate = (d_hidden * upper * sigma * (1.0 + gate * (1.0 - sigma))).astype(BF16)
+        d_up = (d_hidden * active).astype(BF16)
+        d_in = jnp.concatenate([d_gate, d_up], axis=1)
+
+        def partial_sum(w_o, w_i):
+            out = dot(hidden, w_o, 1, 0).astype(BF16)
+            back = dot(d_in, w_i, 1, 1).astype(BF16)
+            value = jnp.concatenate([out, back], axis=1).reshape(count, 2, tok_count, 2 * share)
+            arrived = lax.ppermute(value[:, 1], "ep", other_core)
+            return value[:, 0].astype(F32) + arrived.astype(F32)
+
+        sent = partial_sum(w_out_other, w_in_other).astype(BF16)
+        arrived = lax.ppermute(sent, "tp", other_share)
+        total = partial_sum(w_out_mine, w_in_mine) + arrived.astype(F32)
+        return x, cot, hidden, d_gate, d_up, d_combine_part, total.astype(BF16)
+
+    both_in = jnp.concatenate([tokens, cotangent], axis=1)
+    groups = [group_pass([both_in], 0)]
+    right, left = both_in, both_in
+    for step in range(1, half):
+        right = lax.ppermute(right, "ep", forward)
+        left = lax.ppermute(left, "ep", backward)
+        groups.append(group_pass([right, left], 4 * step - 2))
+    right = lax.ppermute(right[:, :width], "ep", forward)
+    left = lax.ppermute(left[:, width:], "ep", backward)
+    groups.append(group_pass([jnp.concatenate([right, left], axis=1)], 4 * half - 2))
+
+    x, cot, hidden, d_gate, d_up, d_combine_part = (
+        jnp.concatenate([group[i] for group in groups], axis=0) for i in range(6)
+    )
+    totals = {0: groups[0][6][0], half: groups[half][6][0]}
+    for step in range(1, half):
+        totals[-step], totals[step] = groups[step][6][0], groups[step][6][1]
+
+    up_sum, down_sum = totals[half][:, :share], totals[half][:, share:]
+    up_sum = jnp.pad(lax.ppermute(up_sum, "ep", forward).astype(F32), ((0, 0), (0, share)))
+    down_sum = jnp.pad(lax.ppermute(down_sum, "ep", backward).astype(F32), ((0, 0), (share, 0)))
+    for step in range(half - 1, 0, -1):
+        up_sum = (totals[step].astype(F32) + up_sum).astype(BF16)
+        down_sum = (totals[-step].astype(F32) + down_sum).astype(BF16)
+        up_sum = lax.ppermute(up_sum, "ep", forward).astype(F32)
+        down_sum = lax.ppermute(down_sum, "ep", backward).astype(F32)
+    home = (totals[0].astype(F32) + up_sum + down_sum).astype(BF16)
+    mixed, d_tokens = home[:, :share], home[:, share:]
+
+    spread = jnp.sum(jnp.where(chosen, d_combine_part.reshape(ep_count, tok_count, per_device)[..., None], 0.0), axis=2)
+    spread = jnp.take(spread, spot, axis=0).reshape(ep_count * tok_count, top_k)
+    d_combine = lax.psum(lax.psum_scatter(spread, "ep", scatter_dimension=0, tiled=True), "tp")
+
+    tail = slice(last * units, (last + 1) * units)
+    packed = jnp.concatenate([hidden[:, tail], d_gate[:, tail], d_up[:, tail]], axis=1)
+    packed = packed.reshape(ep_count, tok_count, 3 * units)
+    packed = jnp.einsum("brt,btf->brf", rows_of(experts[last]), packed, preferred_element_type=F32).astype(BF16)
+    swapped = jnp.take(lax.ppermute(packed, "ep", partners), from_partner, axis=0)
+    packed = jnp.where(my_move, swapped, packed)
+    spread_rows = jnp.einsum("brt,brf->btf", rows_of(new_last), packed, preferred_element_type=F32).astype(BF16)
+    spread_rows = spread_rows.reshape(ep_count * tok_count, 3 * units)
+
+    def grads(left_side, own, moved):
+        parts = [left_side(own[:, l * units : (l + 1) * units]) for l in range(last)] + [left_side(moved)]
+        return jnp.stack(parts)
+
+    grad_gate = grads(lambda v: dot(x, v, 0, 0).astype(BF16), d_gate, spread_rows[:, units : 2 * units])
+    grad_up = grads(lambda v: dot(x, v, 0, 0).astype(BF16), d_up, spread_rows[:, 2 * units :])
+    grad_down = grads(lambda v: dot(v, cot, 0, 0).astype(BF16), hidden, spread_rows[:, :units])
+    return (mixed, d_tokens, d_combine, grad_gate, grad_up, grad_down)
+
+
+def exchange_halves(value, axis, distance):
     mask = 2**distance
     pairs = [(source, source ^ mask) for source in range(lax.axis_size(axis))]
     return lax.ppermute(value, axis, pairs)
 
 
-def body(tokens, expert_ids, combine, cotangent, old_layout, pair_moves, gate_w, up_w, down_w):
+def dispatch_body(tokens, expert_ids, combine, cotangent, old_layout, pair_moves, gate_w, up_w, down_w):
     ep_count = lax.axis_size("ep")
     tp_count = lax.axis_size("tp")
     tok_count, top_k = expert_ids.shape
@@ -35,7 +207,7 @@
         jnp.where(source_slot[:, None] == slot_ids[None, :], old_layout[None, :], 0), axis=1
     )
     w_gate, w_up, w_down = (gate_w, up_w, down_w)
-    arrived = from_partner(
+    arrived = exchange_halves(
         (gate_w[per_device - 1], up_w[per_device - 1], down_w[per_device - 1]), "ep", swap_bit
     )
     w_gate = jnp.concatenate(
@@ -116,6 +288,14 @@
     return (mixed, d_tokens, d_combine, grad_gate, grad_up, grad_down)
 
 
+def body(*operands):
+    expert_ids, old_layout = operands[1], operands[4]
+    tok_count, top_k = expert_ids.shape
+    ep_count = lax.axis_size("ep")
+    rows = 3 * tok_count * top_k * ep_count // (2 * old_layout.shape[0]) * operands[6].shape[0]
+    return (gather_body if ep_count * tok_count <= 2 * rows else dispatch_body)(*operands)
+
+
 def solution(mesh):
     return jax.shard_map(
         body,

time: 853 us -> 501 us (0.59)
  the two profiles are of different devices: /device:TPU:16 before, /device:TPU:0 now
where the time goes in v1:
time: 501 us; the launch traced here: 494 us
  waiting for transfers between devices  119 us (24%)
  matrix products  112 us (22%)
  local copies, waits for them, and re-layouts  96.8 us (19%)
  other arithmetic  78.3 us (16%)
  blocking collectives  42.8 us (9%)
  starting transfers between devices  27.3 us (5%)
  between operations  17.5 us (3%)
    dot_general x36, matrix products, dot(): lax.dot_general(a, b, (((ca,), (cb,)), ((), ())), preferred_element_type=...  105 us
    reduce_scatter x1, waiting for transfers between devices, gather_body(): lax.psum_scatter(spread, 'ep', scatter_dimension=0, tiled=True)  43.7 us
    unnamed x185, local copies, waits for them, and re-layouts  42.4 us
    all_gather x1, blocking collectives, gather_body(): lax.all_gather(jnp.concatenate([expert_ids.astype(F32), combine], axis=1)...  36.7 us
    ppermute x3, waiting for transfers between devices, gather_body(): right = lax.ppermute(right, 'ep', forward)  31.5 us
    ppermute x5, waiting for transfers between devices, group_pass(): arrived = lax.ppermute(sent, 'tp', other_share)  27.6 us
    another operation x8, other arithmetic, group_pass(): jnp.stack([near, far], axis=1).reshape(count * 2 * tok_count, 2 * width)  22 us
    reshape x5, local copies, waits for them, and re-layouts, group_pass(): (hidden * pulled).reshape(-1, per_device, units)  14.1 us
  transfers between devices with their start and end apart: 38, of which 13 were waited for; matrix products, arithmetic and copies ran while one was open for 33% of the time, Pallas kernels for 0%

profile of v1, /device:TPU:0, one launch (start us, length us, event | category | flops | bytes accessed | tf_op | source)
XLA Modules:
  0.0 493.5 jit_solution(14243606381975635902)
XLA Ops:
  16.4 36.7 %all-gather = f32[2048,16]{0,1:T(8,128)S(1)} all-gather(f32[128,16]{0,1:T(8,128)S(1)} %pad_maximum_fusion.38), channel_id=2, replica_groups=mesh['ep'=16,'tp'=2] {'ep'}, dimensions={0}, use_global_device_ids=true | all-gather | bytes 139264 | tf_op jit(solution)/shard_map/all_gather | solution.py:64
  63.0 5.7 %slice_bitcast_fusion.1 = (bf16[2048,384]{1,0:T(8,128)(2,1)}, bf16[2048,384]{1,0:T(8,128)(2,1)}, bf16[2048,384]{1,0:T(8,128)(2,1)}, bf16[2048,384]{1,0:T(8,128)(2,1)}) fusion(bf16[2,2048,384]{2,1,0:T(8,128)(2,1)} %param.19, bf16[2,2048,384]{2,1,0:T(8,128)(2,1)} %param.18), kind=kLoop, calls=%fused_computation.118 | loop fusion | bytes 12582912 | tf_op jit(solution)/shard_map/squeeze | solution.py:86
  69.9 3.5 pad_maximum_fusion
  73.5 5.4 %fusion.178 = (bf16[2,1,128,4096]{3,2,1,0:T(8,128)(2,1)}, bf16[2,128,4096]{2,1,0:T(8,128)(2,1)}) fusion(bf16[1,128,4096]{2,1,0:T(8,128)(2,1)} %bitcast.21, bf16[1,128,4096]{2,1,0:T(8,128)(2,1)} %bitcast.20), kind=kLoop, calls=%fused_computation.346 | loop fusion | flops 1048576 | bytes 6291456 | tf_op jit(solution)/shard_map/stack | solution.py:98
  91.2 15.4 %collective-permute-done.10 = bf16[128,4096]{1,0:T(8,128)(2,1)} collective-permute-done((bf16[128,4096]{1,0:T(8,128)(2,1)}, bf16[128,4096]{1,0:T(8,128)(2,1)}, u32[]{:S(2)}, u32[]{:S(2)}) %collective-permute-start.10) | collective-permute-done | bytes 1048608 | tf_op jit(solution)/shard_map/ppermute | solution.py:131
  111.3 3.8 fusion.177
  115.1 16.1 %collective-permute-done.16 = bf16[128,4096]{1,0:T(8,128)(2,1)S(1)} collective-permute-done((bf16[128,4096]{1,0:T(8,128)(2,1)}, bf16[128,4096]{1,0:T(8,128)(2,1)S(1)}, u32[]{:S(2)}, u32[]{:S(2)}) %collective-permute-start.16) | collective-permute-done | bytes 1048608 | tf_op jit(solution)/shard_map/ppermute | solution.py:131
  141.4 3.4 fusion.25
  144.8 3.6 fusion.125
  150.2 3.3 copy-done.61
  168.0 3.4 fusion.21
  171.5 3.6 fusion.126
  175.0 3.1 reshape.336
  181.6 4.8 slice_dynamic-update-slice_fusion.2
  188.1 5.3 %fusion.106 = f32[256,1536]{1,0:T(8,128)S(1)} fusion(bf16[2048,1536]{1,0:T(8,128)(2,1)} %copy-done.21, bf16[256,4096]{1,0:T(8,128)(2,1)S(1)} %bitcast.307), kind=kOutput, calls=%fused_computation.191 | convolution fusion | flops 1610612736 | bytes 8912896 | tf_op jit(solution)/shard_map/dot_general | solution.py:42
  205.2 3.4 fusion.17
  208.6 3.6 fusion.127
  212.2 3.2 reshape.337
  248.2 9.7 %fusion.2 = bf16[1,2048,384]{2,1,0:T(8,128)(2,1)} fusion(bf16[2048,2048]{1,0:T(8,128)(2,1)} %get-tuple-element.81, bf16[2048,768]{1,0:T(8,128)(2,1)S(1)} %get-tuple-element.72), kind=kOutput, calls=%fused_computation.21 | convolution fusion | flops 3222011904 | bytes 11534336 | tf_op jit(solution)/shard_map/dot_general | solution.py:42
  257.9 9.3 %fusion = bf16[1,2048,384]{2,1,0:T(8,128)(2,1)} fusion(bf16[2048,2048]{1,0:T(8,128)(2,1)} %get-tuple-element.81, bf16[2048,768]{1,0:T(8,128)(2,1)S(1)} %get-tuple-element.74), kind=kOutput, calls=%fused_computation.19 | convolution fusion | flops 3222011904 | bytes 11534336 | tf_op jit(solution)/shard_map/dot_general | solution.py:42
  296.8 8.1 %fusion.4 = bf16[1,384,2048]{2,1,0:T(8,128)(2,1)} fusion(bf16[2048,2048]{1,0:T(8,128)(2,1)} %get-tuple-element.80, bf16[2048,768]{1,0:T(8,128)(2,1)S(1)} %get-tuple-element.10), kind=kOutput, calls=%fused_computation.23 | convolution fusion | flops 3222011904 | bytes 11534336 | tf_op jit(solution)/shard_map/dot_general | solution.py:42
  331.9 43.7 %reduce-scatter.2.cloned.1.call-done = f32[128,8]{0,1:T(8,128)} async-done(((f32[2048,8]{0,1:T(8,128)}), f32[128,8]{0,1:T(8,128)}) %reduce-scatter.2.cloned.1.call-update) | async-done | bytes 4112 | tf_op jit(solution)/shard_map/reduce_scatter | solution.py:158
  375.5 6.0 %psum.7 = f32[128,8]{0,1:T(8,128)} all-reduce(f32[128,8]{0,1:T(8,128)} %reduce-scatter.2.cloned.1.call-done), channel_id=1, replica_groups=mesh['ep'=16,'tp'=2] {'tp'}, use_global_device_ids=true, to_apply=%region_8.9 | all-reduce | flops 1024 | bytes 8192 | tf_op jit(solution)/shard_map/psum | solution.py:158
  393.5 3.5 gather_fusion.2
  397.1 3.1 convolution_convert_fusion
  400.2 8.1 %fusion.3 = bf16[1,2048,384]{2,1,0:T(8,128)(2,1)S(1)} fusion(bf16[2048,2048]{1,0:T(8,128)(2,1)} %get-tuple-element.81, bf16[2048,1152]{1,0:T(8,128)(2,1)S(1)} %bitcast.327), kind=kOutput, calls=%fused_computation.22 | convolution fusion | flops 3222011904 | bytes 11534336 | tf_op jit(solution)/shard_map/dot_general | solution.py:42
  408.3 4.9 fusion.1
  413.3 3.6 fusion.5
  420.8 17.5 %collective-permute-done.21 = bf16[2,128,2048]{2,1,0:T(8,128)(2,1)} collective-permute-done((bf16[2,128,2048]{2,1,0:T(8,128)(2,1)}, bf16[2,128,2048]{2,1,0:T(8,128)(2,1)}, u32[]{:S(2)}, u32[]{:S(2)}) %collective-permute-start.21) | collective-permute-done | bytes 1048608 | tf_op jit(solution)/shard_map/ppermute | solution.py:123
  441.9 4.1 collective-permute-done.32
  451.9 8.1 %collective-permute-done.29 = bf16[128,2048]{1,0:T(8,128)(2,1)S(1)} collective-permute-done((bf16[128,2048]{1,0:T(8,128)(2,1)S(1)}, bf16[128,2048]{1,0:T(8,128)(2,1)S(1)}, u32[]{:S(2)}, u32[]{:S(2)}) %collective-permute-start.29) | collective-permute-done | bytes 524320 | tf_op jit(solution)/shard_map/ppermute | solution.py:151
  463.4 8.7 %collective-permute-done.9 = bf16[2,128,2048]{2,1,0:T(8,128)(2,1)S(1)} collective-permute-done((bf16[2,128,2048]{2,1,0:T(8,128)(2,1)S(1)}, bf16[2,128,2048]{2,1,0:T(8,128)(2,1)S(1)}, u32[]{:S(2)}, u32[]{:S(2)}) %collective-permute-start.9) | collective-permute-done | bytes 1048608 | tf_op jit(solution)/shard_map/ppermute | solution.py:123
  (393 shorter events, 210.3 us)
Async XLA Ops:
  7.2 368.3 %reduce-scatter.2.cloned.1.call-start = ((), (), s32[]{:S(2)}) async-start(), calls=%async_computation.1 | async-start | bytes 69632 | tf_op jit(solution)/shard_map/reduce_scatter | solution.py:158
  11.2 62.2 %collective-permute-start.4 = (bf16[128,4096]{1,0:T(8,128)(2,1)}, bf16[128,4096]{1,0:T(8,128)(2,1)}, u32[]{:S(2)}, u32[]{:S(2)}) collective-permute-start(bf16[128,4096]{1,0:T(8,128)(2,1)} %constant_dynamic-update-slice_fusion), channel_id=1, source_target_pairs={{0,8},{2,10},{8,16},{10,18},{16,24},{18,26},{24,28},{26,30},{28,20... | collective-permute-start | bytes 3145736 | tf_op jit(solution)/shard_map/ppermute | solution.py:131
  14.3 59.2 %collective-permute-start.5 = (bf16[128,4096]{1,0:T(8,128)(2,1)}, bf16[128,4096]{1,0:T(8,128)(2,1)}, u32[]{:S(2)}, u32[]{:S(2)}) collective-permute-start(bf16[128,4096]{1,0:T(8,128)(2,1)} %constant_dynamic-update-slice_fusion), channel_id=1, source_target_pairs={{0,4},{2,6},{8,0},{10,2},{16,8},{18,10},{24,16},{26,18},{28,24},{3... | collective-permute-start | bytes 3145736 | tf_op jit(solution)/shard_map/ppermute | solution.py:132
  14.3 64.9 %collective-permute-start = (bf16[1,128,4096]{2,1,0:T(8,128)(2,1)}, bf16[1,128,4096]{2,1,0:T(8,128)(2,1)}, u32[]{:S(2)}, u32[]{:S(2)}) collective-permute-start(bf16[1,128,4096]{2,1,0:T(8,128)(2,1)} %bitcast.1), channel_id=1, source_target_pairs={{0,2},{2,0},{4,6},{6,4},{8,10},{10,8},{12,14},{14,12},{16,18},{18,... | collective-permute-start | bytes 3145736 | tf_op jit(solution)/shard_map/ppermute | solution.py:96
  78.9 59.1 %collective-permute-start.6 = (bf16[2,128,4096]{2,1,0:T(8,128)(2,1)}, bf16[2,128,4096]{2,1,0:T(8,128)(2,1)}, u32[]{:S(2)}, u32[]{:S(2)}) collective-permute-start(bf16[2,128,4096]{2,1,0:T(8,128)(2,1)} %get-tuple-element.89), channel_id=1, source_target_pairs={{0,2},{2,0},{4,6},{6,4},{8,10},{10,8},{12,14},{14,12},{16,18},{18,... | collective-permute-start | bytes 6291464 | tf_op jit(solution)/shard_map/ppermute | solution.py:96
  81.0 25.6 %collective-permute-start.10 = (bf16[128,4096]{1,0:T(8,128)(2,1)}, bf16[128,4096]{1,0:T(8,128)(2,1)}, u32[]{:S(2)}, u32[]{:S(2)}) collective-permute-start(bf16[128,4096]{1,0:T(8,128)(2,1)} %collective-permute-done.4), channel_id=1, source_target_pairs={{0,8},{2,10},{8,16},{10,18},{16,24},{18,26},{24,28},{26,30},{28,20... | collective-permute-start | bytes 3145736 | tf_op jit(solution)/shard_map/ppermute | solution.py:131
  81.0 25.8 %collective-permute-start.11 = (bf16[128,4096]{1,0:T(8,128)(2,1)}, bf16[128,4096]{1,0:T(8,128)(2,1)}, u32[]{:S(2)}, u32[]{:S(2)}) collective-permute-start(bf16[128,4096]{1,0:T(8,128)(2,1)} %collective-permute-done.5), channel_id=1, source_target_pairs={{0,4},{2,6},{8,0},{10,2},{16,8},{18,10},{24,16},{26,18},{28,24},{3... | collective-permute-start | bytes 3145736 | tf_op jit(solution)/shard_map/ppermute | solution.py:132
  106.6 24.6 %collective-permute-start.16 = (bf16[128,4096]{1,0:T(8,128)(2,1)}, bf16[128,4096]{1,0:T(8,128)(2,1)S(1)}, u32[]{:S(2)}, u32[]{:S(2)}) collective-permute-start(bf16[128,4096]{1,0:T(8,128)(2,1)} %collective-permute-done.10), channel_id=1, source_target_pairs={{0,8},{2,10},{8,16},{10,18},{16,24},{18,26},{24,28},{26,30},{28,20... | collective-permute-start | bytes 3145736 | tf_op jit(solution)/shard_map/ppermute | solution.py:131
  106.8 24.7 %collective-permute-start.17 = (bf16[128,4096]{1,0:T(8,128)(2,1)}, bf16[128,4096]{1,0:T(8,128)(2,1)S(1)}, u32[]{:S(2)}, u32[]{:S(2)}) collective-permute-start(bf16[128,4096]{1,0:T(8,128)(2,1)} %collective-permute-done.11), channel_id=1, source_target_pairs={{0,4},{2,6},{8,0},{10,2},{16,8},{18,10},{24,16},{26,18},{28,24},{3... | collective-permute-start | bytes 3145736 | tf_op jit(solution)/shard_map/ppermute | solution.py:132
  115.1 48.8 %collective-permute-start.12 = (bf16[2,128,4096]{2,1,0:T(8,128)(2,1)}, bf16[2,128,4096]{2,1,0:T(8,128)(2,1)}, u32[]{:S(2)}, u32[]{:S(2)}) collective-permute-start(bf16[2,128,4096]{2,1,0:T(8,128)(2,1)} %get-tuple-element.87), channel_id=1, source_target_pairs={{0,2},{2,0},{4,6},{6,4},{8,10},{10,8},{12,14},{14,12},{16,18},{18,... | collective-permute-start | bytes 6291464 | tf_op jit(solution)/shard_map/ppermute | solution.py:96
  133.8 66.7 %collective-permute-start.18 = (bf16[2,128,4096]{2,1,0:T(8,128)(2,1)}, bf16[2,128,4096]{2,1,0:T(8,128)(2,1)}, u32[]{:S(2)}, u32[]{:S(2)}) collective-permute-start(bf16[2,128,4096]{2,1,0:T(8,128)(2,1)} %get-tuple-element.85), channel_id=1, source_target_pairs={{0,2},{2,0},{4,6},{6,4},{8,10},{10,8},{12,14},{14,12},{16,18},{18,... | collective-permute-start | bytes 6291464 | tf_op jit(solution)/shard_map/ppermute | solution.py:96
  134.6 25.5 %collective-permute-start.22 = (bf16[128,2048]{1,0:T(8,128)(2,1)}, bf16[128,2048]{1,0:T(8,128)(2,1)}, u32[]{:S(2)}, u32[]{:S(2)}) collective-permute-start(bf16[128,2048]{1,0:T(8,128)(2,1)} %slice.340), channel_id=1, source_target_pairs={{0,8},{2,10},{8,16},{10,18},{16,24},{18,26},{24,28},{26,30},{28,20... | collective-permute-start | bytes 1572872 | tf_op jit(solution)/shard_map/ppermute | solution.py:134
  135.7 26.3 %collective-permute-start.23 = (bf16[128,2048]{1,0:T(8,128)(2,1)}, bf16[128,2048]{1,0:T(8,128)(2,1)}, u32[]{:S(2)}, u32[]{:S(2)}) collective-permute-start(bf16[128,2048]{1,0:T(8,128)(2,1)} %slice.341), channel_id=1, source_target_pairs={{0,4},{2,6},{8,0},{10,2},{16,8},{18,10},{24,16},{26,18},{28,24},{3... | collective-permute-start | bytes 1572872 | tf_op jit(solution)/shard_map/ppermute | solution.py:135
  163.9 22.5 %collective-permute-start.24 = (bf16[1,128,4096]{2,1,0:T(8,128)(2,1)}, bf16[1,128,4096]{2,1,0:T(8,128)(2,1)}, u32[]{:S(2)}, u32[]{:S(2)}) collective-permute-start(bf16[1,128,4096]{2,1,0:T(8,128)(2,1)} %bitcast.61), channel_id=1, source_target_pairs={{0,2},{2,0},{4,6},{6,4},{8,10},{10,8},{12,14},{14,12},{16,18},{18,... | collective-permute-start | bytes 3145736 | tf_op jit(solution)/shard_map/ppermute | solution.py:96
  307.7 85.2 %collective-permute-start.36 = (bf16[16,48,1152]{2,1,0:T(8,128)(2,1)}, bf16[16,48,1152]{2,1,0:T(8,128)(2,1)}, u32[]{:S(2)}, u32[]{:S(2)}) collective-permute-start(bf16[16,48,1152]{2,1,0:T(8,128)(2,1)} %convolution_convert_fusion.1), channel_id=1, source_target_pairs={{0,16},{2,18},{4,20},{6,22},{8,24},{10,26},{12,28},{14,30},{16,0},... | collective-permute-start | bytes 5308424 | tf_op jit(solution)/shard_map/ppermute | solution.py:164
  308.9 170.6 %collective-permute-start.1 = (bf16[1,128,2048]{2,1,0:T(8,128)(2,1)}, bf16[1,128,2048]{2,1,0:T(8,128)(2,1)}, u32[]{:S(2)}, u32[]{:S(2)}) collective-permute-start(bf16[1,128,2048]{2,1,0:T(8,128)(2,1)} %slice_bitcast_fusion.28), channel_id=1, source_target_pairs={{0,2},{2,0},{4,6},{6,4},{8,10},{10,8},{12,14},{14,12},{16,18},{18,... | collective-permute-start | bytes 1572872 | tf_op jit(solution)/shard_map/ppermute | solution.py:119
  310.7 70.9 %collective-permute-start.2 = (bf16[1,128,2048]{2,1,0:T(8,128)(2,1)}, bf16[1,128,2048]{2,1,0:T(8,128)(2,1)}, u32[]{:S(2)}, u32[]{:S(2)}) collective-permute-start(bf16[1,128,2048]{2,1,0:T(8,128)(2,1)} %slice_bitcast_fusion.26), channel_id=1, source_target_pairs={{0,2},{2,0},{4,6},{6,4},{8,10},{10,8},{12,14},{14,12},{16,18},{18,... | collective-permute-start | bytes 1572872 | tf_op jit(solution)/shard_map/ppermute | solution.py:119
  319.6 64.3 %collective-permute-start.25 = (bf16[1,128,2048]{2,1,0:T(8,128)(2,1)}, bf16[1,128,2048]{2,1,0:T(8,128)(2,1)}, u32[]{:S(2)}, u32[]{:S(2)}) collective-permute-start(bf16[1,128,2048]{2,1,0:T(8,128)(2,1)} %slice_bitcast_fusion.21), channel_id=1, source_target_pairs={{0,2},{2,0},{4,6},{6,4},{8,10},{10,8},{12,14},{14,12},{16,18},{18,... | collective-permute-start | bytes 1572872 | tf_op jit(solution)/shard_map/ppermute | solution.py:119
  329.3 55.0 %collective-permute-start.27 = (bf16[1,128,2048]{2,1,0:T(8,128)(2,1)}, bf16[1,128,2048]{2,1,0:T(8,128)(2,1)}, u32[]{:S(2)}, u32[]{:S(2)}) collective-permute-start(bf16[1,128,2048]{2,1,0:T(8,128)(2,1)} %fusion.93), channel_id=1, source_target_pairs={{0,1},{1,0},{2,3},{3,2},{4,5},{5,4},{6,7},{7,6},{8,9},{9,8},{10,11... | collective-permute-start | bytes 1572872 | tf_op jit(solution)/shard_map/ppermute | solution.py:123
  383.9 63.8 %collective-permute-start.13 = (bf16[2,128,2048]{2,1,0:T(8,128)(2,1)}, bf16[2,128,2048]{2,1,0:T(8,128)(2,1)}, u32[]{:S(2)}, u32[]{:S(2)}) collective-permute-start(bf16[2,128,2048]{2,1,0:T(8,128)(2,1)} %slice_bitcast_fusion.10), channel_id=1, source_target_pairs={{0,2},{2,0},{4,6},{6,4},{8,10},{10,8},{12,14},{14,12},{16,18},{18,... | collective-permute-start | bytes 3145736 | tf_op jit(solution)/shard_map/ppermute | solution.py:119
  388.5 30.4 %collective-permute-start.19 = (bf16[2,128,2048]{2,1,0:T(8,128)(2,1)}, bf16[2,128,2048]{2,1,0:T(8,128)(2,1)}, u32[]{:S(2)}, u32[]{:S(2)}) collective-permute-start(bf16[2,128,2048]{2,1,0:T(8,128)(2,1)} %slice_bitcast_fusion.6), channel_id=1, source_target_pairs={{0,2},{2,0},{4,6},{6,4},{8,10},{10,8},{12,14},{14,12},{16,18},{18,... | collective-permute-start | bytes 3145736 | tf_op jit(solution)/shard_map/ppermute | solution.py:119
  390.0 59.0 %collective-permute-start.15 = (bf16[2,128,2048]{2,1,0:T(8,128)(2,1)}, bf16[2,128,2048]{2,1,0:T(8,128)(2,1)}, u32[]{:S(2)}, u32[]{:S(2)}) collective-permute-start(bf16[2,128,2048]{2,1,0:T(8,128)(2,1)} %fusion.9), channel_id=1, source_target_pairs={{0,1},{1,0},{2,3},{3,2},{4,5},{5,4},{6,7},{7,6},{8,9},{9,8},{10,11... | collective-permute-start | bytes 3145736 | tf_op jit(solution)/shard_map/ppermute | solution.py:123
  392.9 45.3 %collective-permute-start.21 = (bf16[2,128,2048]{2,1,0:T(8,128)(2,1)}, bf16[2,128,2048]{2,1,0:T(8,128)(2,1)}, u32[]{:S(2)}, u32[]{:S(2)}) collective-permute-start(bf16[2,128,2048]{2,1,0:T(8,128)(2,1)} %fusion.6), channel_id=1, source_target_pairs={{0,1},{1,0},{2,3},{3,2},{4,5},{5,4},{6,7},{7,6},{8,9},{9,8},{10,11... | collective-permute-start | bytes 3145736 | tf_op jit(solution)/shard_map/ppermute | solution.py:123
  418.9 22.9 %collective-permute-start.28 = (bf16[128,1024]{1,0:T(8,128)(2,1)S(1)}, bf16[128,1024]{1,0:T(8,128)(2,1)S(1)}, u32[]{:S(2)}, u32[]{:S(2)}) collective-permute-start(bf16[128,1024]{1,0:T(8,128)(2,1)S(1)} %copy-done.60), channel_id=1, source_target_pairs={{0,8},{2,10},{8,16},{10,18},{16,24},{18,26},{24,28},{26,30},{28,20... | collective-permute-start | bytes 786440 | tf_op jit(solution)/shard_map/ppermute | solution.py:146
  441.8 20.4 %collective-permute-start.7 = (bf16[2,128,2048]{2,1,0:T(8,128)(2,1)S(1)}, bf16[2,128,2048]{2,1,0:T(8,128)(2,1)S(1)}, u32[]{:S(2)}, u32[]{:S(2)}) collective-permute-start(bf16[2,128,2048]{2,1,0:T(8,128)(2,1)S(1)} %copy-done.49), channel_id=1, source_target_pairs={{0,2},{2,0},{4,6},{6,4},{8,10},{10,8},{12,14},{14,12},{16,18},{18,... | collective-permute-start | bytes 3145736 | tf_op jit(solution)/shard_map/ppermute | solution.py:119
  446.0 26.1 %collective-permute-start.9 = (bf16[2,128,2048]{2,1,0:T(8,128)(2,1)S(1)}, bf16[2,128,2048]{2,1,0:T(8,128)(2,1)S(1)}, u32[]{:S(2)}, u32[]{:S(2)}) collective-permute-start(bf16[2,128,2048]{2,1,0:T(8,128)(2,1)S(1)} %copy-done.48), channel_id=1, source_target_pairs={{0,1},{1,0},{2,3},{3,2},{4,5},{5,4},{6,7},{7,6},{8,9},{9,8},{10,11... | collective-permute-start | bytes 3145736 | tf_op jit(solution)/shard_map/ppermute | solution.py:123
  447.7 12.2 %collective-permute-start.29 = (bf16[128,2048]{1,0:T(8,128)(2,1)S(1)}, bf16[128,2048]{1,0:T(8,128)(2,1)S(1)}, u32[]{:S(2)}, u32[]{:S(2)}) collective-permute-start(bf16[128,2048]{1,0:T(8,128)(2,1)S(1)} %get-tuple-element.94), channel_id=1, source_target_pairs={{0,8},{2,10},{8,16},{10,18},{16,24},{18,26},{24,28},{26,30},{28,20... | collective-permute-start | bytes 1572872 | tf_op jit(solution)/shard_map/ppermute | solution.py:151
  449.0 11.9 %collective-permute-start.33 = (bf16[128,2048]{1,0:T(8,128)(2,1)S(1)}, bf16[128,2048]{1,0:T(8,128)(2,1)S(1)}, u32[]{:S(2)}, u32[]{:S(2)}) collective-permute-start(bf16[128,2048]{1,0:T(8,128)(2,1)S(1)} %get-tuple-element.95), channel_id=1, source_target_pairs={{0,4},{2,6},{8,0},{10,2},{16,8},{18,10},{24,16},{26,18},{28,24},{3... | collective-permute-start | bytes 1572872 | tf_op jit(solution)/shard_map/ppermute | solution.py:152
  459.9 21.0 %collective-permute-start.3 = (bf16[1,128,2048]{2,1,0:T(8,128)(2,1)S(1)}, bf16[1,128,2048]{2,1,0:T(8,128)(2,1)S(1)}, u32[]{:S(2)}, u32[]{:S(2)}) collective-permute-start(bf16[1,128,2048]{2,1,0:T(8,128)(2,1)S(1)} %copy-done.56), channel_id=1, source_target_pairs={{0,1},{1,0},{2,3},{3,2},{4,5},{5,4},{6,7},{7,6},{8,9},{9,8},{10,11... | collective-permute-start | bytes 1572872 | tf_op jit(solution)/shard_map/ppermute | solution.py:123
  461.3 11.4 %collective-permute-start.30 = (bf16[128,2048]{1,0:T(8,128)(2,1)S(1)}, bf16[128,2048]{1,0:T(8,128)(2,1)S(1)}, u32[]{:S(2)}, u32[]{:S(2)}) collective-permute-start(bf16[128,2048]{1,0:T(8,128)(2,1)S(1)} %get-tuple-element.92), channel_id=1, source_target_pairs={{0,8},{2,10},{8,16},{10,18},{16,24},{18,26},{24,28},{26,30},{28,20... | collective-permute-start | bytes 1572872 | tf_op jit(solution)/shard_map/ppermute | solution.py:151
  462.3 10.7 %collective-permute-start.34 = (bf16[128,2048]{1,0:T(8,128)(2,1)S(1)}, bf16[128,2048]{1,0:T(8,128)(2,1)S(1)}, u32[]{:S(2)}, u32[]{:S(2)}) collective-permute-start(bf16[128,2048]{1,0:T(8,128)(2,1)S(1)} %get-tuple-element.93), channel_id=1, source_target_pairs={{0,4},{2,6},{8,0},{10,2},{16,8},{18,10},{24,16},{26,18},{28,24},{3... | collective-permute-start | bytes 1572872 | tf_op jit(solution)/shard_map/ppermute | solution.py:152
  473.4 10.2 %collective-permute-start.31 = (bf16[128,2048]{1,0:T(8,128)(2,1)S(1)}, bf16[128,2048]{1,0:T(8,128)(2,1)S(1)}, u32[]{:S(2)}, u32[]{:S(2)}) collective-permute-start(bf16[128,2048]{1,0:T(8,128)(2,1)S(1)} %get-tuple-element.90), channel_id=1, source_target_pairs={{0,8},{2,10},{8,16},{10,18},{16,24},{18,26},{24,28},{26,30},{28,20... | collective-permute-start | bytes 1572872 | tf_op jit(solution)/shard_map/ppermute | solution.py:151
  (91 other events, 593.4 us)
Sparse Core Ops, SparseCore 0:
  322.8 52.6 reduce-scatter.1

commit v2 on v1

--- a/solution.py
+++ b/solution.py
@@ -61,22 +61,14 @@
     my_share = lax.axis_index("tp")
     arrival, spot, from_partner = (jnp.asarray(table)[me] for table in block_tables(order))
 
-    meta = lax.all_gather(
-        jnp.concatenate([expert_ids.astype(F32), combine], axis=1), "ep", axis=0, tiled=False
-    )
-    meta = jnp.take(meta, arrival, axis=0)
-    ids = meta[:, :, :top_k].astype(jnp.int32)
-    weights = meta[:, :, top_k:]
     my_move = pair_moves[me] == 1
     last = per_device - 1
     experts = lax.dynamic_slice_in_dim(old_layout, me * per_device, per_device, 0)
     partner_last = old_layout[(me ^ (ep_count // 2)) * per_device + last]
     new_last = jnp.where(my_move, partner_last, experts[last])
-    chosen = ids[:, :, None, :] == experts[None, None, :, None]
-    scale = jnp.sum(jnp.where(chosen, weights[:, :, None, :], 0.0), axis=3)
     earlier = (jnp.arange(tok_count)[:, None] < jnp.arange(tok_count)[None, :]).astype(BF16)
 
-    def rows_of(expert):
+    def rows_of(expert, ids):
         named = jnp.any(ids == expert, axis=2)
         position = jnp.dot(named.astype(BF16), earlier, preferred_element_type=F32).astype(jnp.int32)
         wanted = jnp.arange(capacity, dtype=jnp.int32)[None, :, None]
@@ -91,21 +83,43 @@
     w_out_mine = lax.dynamic_slice_in_dim(w_out, mine_at, share, 1)
     w_out_other = lax.dynamic_slice_in_dim(w_out, other_at, share, 1)
 
-    def group_pass(pieces, first):
-        near = jnp.stack(pieces)
+    parts = []
+    rest = combine
+    for _ in range(3):
+        parts.append(lax.reduce_precision(rest, 8, 7))
+        rest = rest - parts[-1]
+    id_parts = [expert_ids // 256, expert_ids % 256]
+    notes = jnp.concatenate([part.astype(BF16) for part in id_parts + parts], axis=1)
+    notes = jnp.pad(notes, ((0, 0), (0, -notes.shape[1] % 128)))
+    payload = jnp.concatenate([tokens, cotangent, notes], axis=1)
+
+    def compute(pieces):
+        near = jnp.concatenate(pieces)
         far = lax.ppermute(near, "ep", other_core)
         count = len(pieces)
-        group = jnp.stack([near, far], axis=1).reshape(count * 2 * tok_count, 2 * width)
-        x, cot = group[:, :width], group[:, width:]
-        gains = scale[first : first + 2 * count].reshape(-1, per_device)
-        gains_wide = jnp.repeat(gains, units, axis=1)
+        near, far = near.reshape(count, tok_count, -1), far.reshape(count, tok_count, -1)
+        group = jnp.stack([near, far], axis=1).reshape(count * 2 * tok_count, -1)
+        x, cot, said = group[:, :width], group[:, width : 2 * width], group[:, 2 * width :].astype(F32)
+        columns = [said[:, i * top_k : (i + 1) * top_k] for i in range(5)]
+        ids = (columns[0] * 256 + columns[1]).astype(jnp.int32)
+        weights = columns[2] + (columns[3] + columns[4])
+        gains = [
+            jnp.sum(jnp.where(ids == experts[l], weights, 0.0), axis=1, keepdims=True) for l in range(per_device)
+        ]
+        gains_wide = jnp.concatenate([jnp.broadcast_to(gain, (gain.shape[0], units)) for gain in gains], axis=1)
         projected = dot(x, w_in, 1, 0)
         pulled = dot(cot, w_out, 1, 1)
         gate, upper = projected[:, :both], projected[:, both:]
         sigma = jax.nn.sigmoid(gate)
         active = gate * sigma
         hidden = active * upper
-        d_combine_part = jnp.sum((hidden * pulled).reshape(-1, per_device, units), axis=2)
+        traded = hidden * pulled
+        d_weights = sum(
+            jnp.where(
+                ids == experts[l], jnp.sum(traded[:, l * units : (l + 1) * units], axis=1, keepdims=True), 0.0
+            )
+            for l in range(per_device)
+        )
         d_hidden = pulled * gains_wide
         hidden = (hidden * gains_wide).astype(BF16)
         d_gate = (d_hidden * upper * sigma * (1.0 + gate * (1.0 - sigma))).astype(BF16)
@@ -120,50 +134,62 @@
             return value[:, 0].astype(F32) + arrived.astype(F32)
 
         sent = partial_sum(w_out_other, w_in_other).astype(BF16)
-        arrived = lax.ppermute(sent, "tp", other_share)
-        total = partial_sum(w_out_mine, w_in_mine) + arrived.astype(F32)
-        return x, cot, hidden, d_gate, d_up, d_combine_part, total.astype(BF16)
-
-    both_in = jnp.concatenate([tokens, cotangent], axis=1)
-    groups = [group_pass([both_in], 0)]
-    right, left = both_in, both_in
+        kept = partial_sum(w_out_mine, w_in_mine).astype(BF16)
+        ids = ids.reshape(2 * count, tok_count, top_k)
+        tail = slice(last * units, (last + 1) * units)
+        packed = jnp.concatenate([hidden[:, tail], d_gate[:, tail], d_up[:, tail]], axis=1)
+        packed = packed.reshape(2 * count, tok_count, 3 * units)
+        packed = jnp.einsum("brt,btf->brf", rows_of(experts[last], ids), packed, preferred_element_type=F32)
+        return (x, cot, hidden, d_gate, d_up, d_weights, ids, packed.astype(BF16)), sent, kept
+
+    kept_groups, totals = [], []
+    right = left = payload
+    pending = None
+    for step in range(half + 1):
+        pieces = [payload] if step == 0 else [right, left] if step < half else [jnp.concatenate([right, left], axis=1)]
+        if step < half - 1:
+            right = lax.ppermute(right, "ep", forward)
+            left = lax.ppermute(left, "ep", backward)
+        elif step == half - 1:
+            right = lax.ppermute(right[:, :width], "ep", forward)
+            left = lax.ppermute(left[:, width:], "ep", backward)
+        if pending is not None:
+            arrived = lax.ppermute(pending[0], "tp", other_share)
+            totals.append((pending[1].astype(F32) + arrived.astype(F32)).astype(BF16))
+        group, sent, kept = compute(pieces)
+        right, left, sent, kept, group, totals = lax.optimization_barrier((right, left, sent, kept, group, totals))
+        kept_groups.append(group)
+        pending = (sent, kept)
+    arrived = lax.ppermute(pending[0], "tp", other_share)
+    totals.append((pending[1].astype(F32) + arrived.astype(F32)).astype(BF16))
+
+    x, cot, hidden, d_gate, d_up, d_weights, ids, packed = (
+        jnp.concatenate([group[i] for group in kept_groups], axis=0) for i in range(8)
+    )
+    by_hop = {0: totals[0][0], half: totals[half][0]}
     for step in range(1, half):
-        right = lax.ppermute(right, "ep", forward)
-        left = lax.ppermute(left, "ep", backward)
-        groups.append(group_pass([right, left], 4 * step - 2))
-    right = lax.ppermute(right[:, :width], "ep", forward)
-    left = lax.ppermute(left[:, width:], "ep", backward)
-    groups.append(group_pass([jnp.concatenate([right, left], axis=1)], 4 * half - 2))
-
-    x, cot, hidden, d_gate, d_up, d_combine_part = (
-        jnp.concatenate([group[i] for group in groups], axis=0) for i in range(6)
-    )
-    totals = {0: groups[0][6][0], half: groups[half][6][0]}
-    for step in range(1, half):
-        totals[-step], totals[step] = groups[step][6][0], groups[step][6][1]
-
-    up_sum, down_sum = totals[half][:, :share], totals[half][:, share:]
+        by_hop[-step], by_hop[step] = totals[step][0], totals[step][1]
+
+    up_sum, down_sum = by_hop[half][:, :share], by_hop[half][:, share:]
     up_sum = jnp.pad(lax.ppermute(up_sum, "ep", forward).astype(F32), ((0, 0), (0, share)))
     down_sum = jnp.pad(lax.ppermute(down_sum, "ep", backward).astype(F32), ((0, 0), (share, 0)))
     for step in range(half - 1, 0, -1):
-        up_sum = (totals[step].astype(F32) + up_sum).astype(BF16)
-        down_sum = (totals[-step].astype(F32) + down_sum).astype(BF16)
+        up_sum = (by_hop[step].astype(F32) + up_sum).astype(BF16)
+        down_sum = (by_hop[-step].astype(F32) + down_sum).astype(BF16)
         up_sum = lax.ppermute(up_sum, "ep", forward).astype(F32)
         down_sum = lax.ppermute(down_sum, "ep", backward).astype(F32)
-    home = (totals[0].astype(F32) + up_sum + down_sum).astype(BF16)
+    home = (by_hop[0].astype(F32) + up_sum + down_sum).astype(BF16)
     mixed, d_tokens = home[:, :share], home[:, share:]
 
-    spread = jnp.sum(jnp.where(chosen, d_combine_part.reshape(ep_count, tok_count, per_device)[..., None], 0.0), axis=2)
-    spread = jnp.take(spread, spot, axis=0).reshape(ep_count * tok_count, top_k)
-    d_combine = lax.psum(lax.psum_scatter(spread, "ep", scatter_dimension=0, tiled=True), "tp")
-
-    tail = slice(last * units, (last + 1) * units)
-    packed = jnp.concatenate([hidden[:, tail], d_gate[:, tail], d_up[:, tail]], axis=1)
-    packed = packed.reshape(ep_count, tok_count, 3 * units)
-    packed = jnp.einsum("brt,btf->brf", rows_of(experts[last]), packed, preferred_element_type=F32).astype(BF16)
+    d_weights = d_weights + lax.ppermute(d_weights, "tp", other_share)
+    d_weights = jnp.take(d_weights.reshape(ep_count, tok_count, top_k), spot, axis=0)
+    d_combine = lax.psum_scatter(
+        d_weights.reshape(ep_count * tok_count, top_k), "ep", scatter_dimension=0, tiled=True
+    )
+
     swapped = jnp.take(lax.ppermute(packed, "ep", partners), from_partner, axis=0)
     packed = jnp.where(my_move, swapped, packed)
-    spread_rows = jnp.einsum("brt,brf->btf", rows_of(new_last), packed, preferred_element_type=F32).astype(BF16)
+    spread_rows = jnp.einsum("brt,brf->btf", rows_of(new_last, ids), packed, preferred_element_type=F32).astype(BF16)
     spread_rows = spread_rows.reshape(ep_count * tok_count, 3 * units)
 
     def grads(left_side, own, moved):

time: 501 us -> 453 us (0.904)
  waiting for transfers between devices: 119 us -> 73.9 us
  blocking collectives: 42.8 us -> 0 us
  starting transfers between devices: 27.3 us -> 69.8 us
  matrix products: 112 us -> 95.4 us
  other arithmetic: 78.3 us -> 86.3 us
  local copies, waits for them, and re-layouts: 96.8 us -> 102 us
    reduce_scatter x1, waiting for transfers between devices: 43.7 us -> 0.01 us  [gather_body(): lax.psum_scatter(d_weights.reshape(ep_count * tok_count, top_k), 'ep', sc...]
    ppermute x3, starting transfers between devices: 3.84 us -> 43.1 us  [gather_body(): up_sum = lax.ppermute(up_sum, 'ep', forward).astype(F32)]
    all_gather x1 -> x0, blocking collectives: 36.7 us -> none  [gather_body(): lax.all_gather(jnp.concatenate([expert_ids.astype(F32), combine], axis=1)...]
    ppermute x3, waiting for transfers between devices: 31.5 us -> 0.01 us  [gather_body(): right = lax.ppermute(right, 'ep', forward)]
    dot_general x36, matrix products: 105 us -> 85.7 us  [dot(): lax.dot_general(a, b, (((ca,), (cb,)), ((), ())), preferred_element_type=...]
    convert_element_type x13 -> x28, other arithmetic: 15.5 us -> 33.8 us  [the longest x4 10 us: gather_body(): totals.append((pending[1].astype(F32) + arrived.astype(F32)).astype(BF16))]
    reshape x12 -> x0, local copies, waits for them, and re-layouts: 14.8 us -> none  [the longest x5 14.1 us: group_pass(): (hidden * pulled).reshape(-1, per_device, units)]
    ppermute x1, waiting for transfers between devices: 0.01 us -> 14.6 us  [gather_body(): lax.ppermute(up_sum, 'ep', forward).astype(F32)]
  transfers between devices with their start and end apart: 38 -> 39, of which waited for: 13 -> 9; matrix products, arithmetic and copies ran while one was open for 33% -> 54% of each run, Pallas kernels for 0% -> 0%
where the time goes in v2:
time: 453 us; the launch traced here: 445 us
  local copies, waits for them, and re-layouts  102 us (23%)
  matrix products  95.4 us (21%)
  other arithmetic  86.3 us (19%)
  waiting for transfers between devices  73.9 us (16%)
  starting transfers between devices  69.8 us (15%)
  between operations  17.8 us (4%)
    dot_general x36, matrix products, dot(): lax.dot_general(a, b, (((ca,), (cb,)), ((), ())), preferred_element_type=...  85.7 us
    unnamed x189, local copies, waits for them, and re-layouts  49.4 us
    ppermute x3, starting transfers between devices, gather_body(): up_sum = lax.ppermute(up_sum, 'ep', forward).astype(F32)  43.1 us
    ppermute x5, waiting for transfers between devices, gather_body(): arrived = lax.ppermute(pending[0], 'tp', other_share)  40.6 us
    another operation x6, other arithmetic, compute(): group = jnp.stack([near, far], axis=1).reshape(count * 2 * tok_count, -1)  15.4 us
    ppermute x1, waiting for transfers between devices, gather_body(): lax.ppermute(up_sum, 'ep', forward).astype(F32)  14.6 us
    slice x5, local copies, waits for them, and re-layouts, compute(): group[:, width:2 * width]  11.3 us
    convert_element_type x4, other arithmetic, gather_body(): totals.append((pending[1].astype(F32) + arrived.astype(F32)).astype(BF16))  10 us
  transfers between devices with their start and end apart: 39, of which 9 were waited for; matrix products, arithmetic and copies ran while one was open for 54% of the time, Pallas kernels for 0%

profile of v2, /device:TPU:0, one launch (start us, length us, event | category | flops | bytes accessed | tf_op | source)
XLA Modules:
  0.0 444.7 jit_solution(5119807067882630681)
XLA Ops:
  11.1 2.8 fusion.221
  13.9 3.0 collective-permute-start
  16.9 4.7 %slice_bitcast_fusion.1 = (bf16[2048,384]{1,0:T(8,128)(2,1)}, bf16[2048,384]{1,0:T(8,128)(2,1)}, bf16[2048,384]{1,0:T(8,128)(2,1)}, bf16[2048,384]{1,0:T(8,128)(2,1)}) fusion(bf16[2,2048,384]{2,1,0:T(8,128)(2,1)S(1)} %copy-done.30, bf16[2,2048,384]{2,1,0:T(8,128)(2,1)} %param.17), kind=kLoop, calls=%fused_computation.110 | loop fusion | bytes 12582912 | tf_op jit(solution)/shard_map/squeeze | solution.py:78
  22.4 3.6 pad_maximum_fusion
  70.0 3.6 collective-permute-done.10
  75.5 2.8 pad_maximum_fusion.1
  78.4 3.4 fusion.219
  123.3 13.2 %collective-permute-done.16 = bf16[2,128,2048]{2,1,0:T(8,128)(2,1)} collective-permute-done((bf16[2,128,2048]{2,1,0:T(8,128)(2,1)}, bf16[2,128,2048]{2,1,0:T(8,128)(2,1)}, u32[]{:S(2)}, u32[]{:S(2)}) %collective-permute-start.16) | collective-permute-done | bytes 1048608 | tf_op jit(solution)/shard_map/ppermute | solution.py:157
  136.5 2.7 add_convert_fusion.2
  139.3 2.8 pad_maximum_fusion.2
  142.2 3.4 fusion.215
  191.2 11.7 %collective-permute-done.22 = bf16[2,128,2048]{2,1,0:T(8,128)(2,1)} collective-permute-done((bf16[2,128,2048]{2,1,0:T(8,128)(2,1)}, bf16[2,128,2048]{2,1,0:T(8,128)(2,1)}, u32[]{:S(2)}, u32[]{:S(2)}) %collective-permute-start.22) | collective-permute-done | bytes 1048608 | tf_op jit(solution)/shard_map/ppermute | solution.py:157
  205.4 2.8 pad_maximum_fusion.3
  208.3 3.4 fusion.211
  226.8 3.0 fusion.232
  250.2 12.2 %collective-permute-done.26 = bf16[2,128,2048]{2,1,0:T(8,128)(2,1)} collective-permute-done((bf16[2,128,2048]{2,1,0:T(8,128)(2,1)}, bf16[2,128,2048]{2,1,0:T(8,128)(2,1)}, u32[]{:S(2)}, u32[]{:S(2)}) %collective-permute-start.26) | collective-permute-done | bytes 1048608 | tf_op jit(solution)/shard_map/ppermute | solution.py:157
  262.4 2.8 add_convert_fusion
  266.9 4.8 %fusion.203 = f32[256,1536]{1,0:T(8,128)S(1)} fusion(bf16[2048,1536]{1,0:T(8,128)(2,1)} %copy-done.7, bf16[256,4224]{1,0:T(8,128)(2,1)S(1)} %bitcast.271), kind=kOutput, calls=%fused_computation.447 | convolution fusion | flops 1610612736 | bytes 8912896 | tf_op jit(solution)/shard_map/dot_general | solution.py:42
  297.3 10.6 %fusion = bf16[1,2048,384]{2,1,0:T(8,128)(2,1)} fusion(bf16[2048,2048]{1,0:T(8,128)(2,1)} %constant_dynamic-update-slice_fusion.18, bf16[2048,768]{1,0:T(8,128)(2,1)} %constant_dynamic-update-slice_fusion.23), kind=kOutput, calls=%fused_computation.16 | convolution fusion | flops 3222011904 | bytes 11534336 | tf_op jit(solution)/shard_map/dot_general | solution.py:42
  308.0 5.6 %fusion.2 = bf16[1,2048,384]{2,1,0:T(8,128)(2,1)} fusion(bf16[2048,2048]{1,0:T(8,128)(2,1)S(1)} %bitcast.321, bf16[2048,768]{1,0:T(8,128)(2,1)S(1)} %constant_dynamic-update-slice_fusion.38), kind=kOutput, calls=%fused_computation.18 | convolution fusion | flops 3222011904 | bytes 11534336 | tf_op jit(solution)/shard_map/dot_general | solution.py:42
  313.8 4.6 %fusion.4 = bf16[1,384,2048]{2,1,0:T(8,128)(2,1)} fusion(bf16[2048,2048]{1,0:T(8,128)(2,1)S(1)} %constant_dynamic-update-slice_fusion.48, bf16[2048,768]{1,0:T(8,128)(2,1)S(1)} %constant_dynamic-update-slice_fusion.43), kind=kOutput, calls=%fused_computation.20 | convolution fusion | flops 3222011904 | bytes 11534336 | tf_op jit(solution)/shard_map/dot_general | solution.py:42
  322.0 14.6 %collective-permute-done.28 = bf16[128,1024]{1,0:T(8,128)(2,1)S(1)} collective-permute-done((bf16[128,1024]{1,0:T(8,128)(2,1)S(1)}, bf16[128,1024]{1,0:T(8,128)(2,1)S(1)}, u32[]{:S(2)}, u32[]{:S(2)}) %collective-permute-start.28) | collective-permute-done | bytes 262176 | tf_op jit(solution)/shard_map/ppermute | solution.py:174
  337.8 39.3 %collective-permute-start.29 = (bf16[128,2048]{1,0:T(8,128)(2,1)}, bf16[128,2048]{1,0:T(8,128)(2,1)}, u32[]{:S(2)}, u32[]{:S(2)}) collective-permute-start(bf16[128,2048]{1,0:T(8,128)(2,1)} %get-tuple-element.222), channel_id=1, source_target_pairs={{0,8},{2,10},{8,16},{10,18},{16,24},{18,26},{24,28},{26,30},{28,20... | collective-permute-start | bytes 1572872 | tf_op jit(solution)/shard_map/ppermute | solution.py:179
  379.3 9.5 %collective-permute-done.29 = bf16[128,2048]{1,0:T(8,128)(2,1)} collective-permute-done((bf16[128,2048]{1,0:T(8,128)(2,1)}, bf16[128,2048]{1,0:T(8,128)(2,1)}, u32[]{:S(2)}, u32[]{:S(2)}) %collective-permute-start.29) | collective-permute-done | bytes 524320 | tf_op jit(solution)/shard_map/ppermute | solution.py:179
  388.8 2.9 collective-permute-done.33
  391.7 2.9 fusion.90
  396.7 3.5 gather_fusion.1
  400.2 3.6 convolution_convert_fusion
  403.8 8.1 %fusion.1 = bf16[1,2048,384]{2,1,0:T(8,128)(2,1)S(1)} fusion(bf16[2048,2048]{1,0:T(8,128)(2,1)} %constant_dynamic-update-slice_fusion.18, bf16[2048,1152]{1,0:T(8,128)(2,1)S(1)} %bitcast.302), kind=kOutput, calls=%fused_computation.17 | convolution fusion | flops 3222011904 | bytes 11534336 | tf_op jit(solution)/shard_map/dot_general | solution.py:42
  412.0 4.7 %fusion.3 = bf16[1,2048,384]{2,1,0:T(8,128)(2,1)S(1)} fusion(bf16[2048,2048]{1,0:T(8,128)(2,1)S(1)} %bitcast.323, bf16[2048,1152]{1,0:T(8,128)(2,1)S(1)} %bitcast.303), kind=kOutput, calls=%fused_computation.19 | convolution fusion | flops 3222011904 | bytes 11534336 | tf_op jit(solution)/shard_map/dot_general | solution.py:42
  416.8 3.8 fusion.5
  430.4 6.1 %collective-permute-done.35 = bf16[128,2048]{1,0:T(8,128)(2,1)S(1)} collective-permute-done((bf16[128,2048]{1,0:T(8,128)(2,1)S(1)}, bf16[128,2048]{1,0:T(8,128)(2,1)S(1)}, u32[]{:S(2)}, u32[]{:S(2)}) %collective-permute-start.35) | collective-permute-done | bytes 524320 | tf_op jit(solution)/shard_map/ppermute | solution.py:180
  (454 shorter events, 220.1 us)
Async XLA Ops:
  7.2 430.4 %reduce-scatter.2.cloned.1.call-start = ((), (), s32[]{:S(2)}) async-start(), calls=%async_computation.1 | async-start | bytes 69632 | tf_op jit(solution)/shard_map/reduce_scatter | solution.py:186
  13.9 29.9 %collective-permute-start = (bf16[128,4224]{1,0:T(8,128)(2,1)}, bf16[128,4224]{1,0:T(8,128)(2,1)}, u32[]{:S(2)}, u32[]{:S(2)}) collective-permute-start(bf16[128,4224]{1,0:T(8,128)(2,1)} %get-tuple-element.217), channel_id=1, source_target_pairs={{0,8},{2,10},{8,16},{10,18},{16,24},{18,26},{24,28},{26,30},{28,20... | collective-permute-start | bytes 3244040 | tf_op jit(solution)/shard_map/ppermute | solution.py:151
  16.9 26.9 %collective-permute-start.1 = (bf16[128,4224]{1,0:T(8,128)(2,1)}, bf16[128,4224]{1,0:T(8,128)(2,1)}, u32[]{:S(2)}, u32[]{:S(2)}) collective-permute-start(bf16[128,4224]{1,0:T(8,128)(2,1)} %get-tuple-element.217), channel_id=1, source_target_pairs={{0,4},{2,6},{8,0},{10,2},{16,8},{18,10},{24,16},{26,18},{28,24},{3... | collective-permute-start | bytes 3244040 | tf_op jit(solution)/shard_map/ppermute | solution.py:152
  16.9 9.1 %collective-permute-start.2 = (bf16[128,4224]{1,0:T(8,128)(2,1)}, bf16[128,4224]{1,0:T(8,128)(2,1)}, u32[]{:S(2)}, u32[]{:S(2)}) collective-permute-start(bf16[128,4224]{1,0:T(8,128)(2,1)} %get-tuple-element.217), channel_id=1, source_target_pairs={{0,2},{2,0},{4,6},{6,4},{8,10},{10,8},{12,14},{14,12},{16,18},{18,... | collective-permute-start | bytes 3244040 | tf_op jit(solution)/shard_map/ppermute | solution.py:98
  48.4 27.1 %collective-permute-start.7 = (bf16[256,4224]{1,0:T(8,128)(2,1)}, bf16[256,4224]{1,0:T(8,128)(2,1)}, u32[]{:S(2)}, u32[]{:S(2)}) collective-permute-start(bf16[256,4224]{1,0:T(8,128)(2,1)} %constant_dynamic-update-slice_fusion.5), channel_id=1, source_target_pairs={{0,2},{2,0},{4,6},{6,4},{8,10},{10,8},{12,14},{14,12},{16,18},{18,... | collective-permute-start | bytes 6488072 | tf_op jit(solution)/shard_map/ppermute | solution.py:98
  57.3 45.3 %collective-permute-start.5 = (bf16[128,4224]{1,0:T(8,128)(2,1)}, bf16[128,4224]{1,0:T(8,128)(2,1)}, u32[]{:S(2)}, u32[]{:S(2)}) collective-permute-start(bf16[128,4224]{1,0:T(8,128)(2,1)} %collective-permute-done), channel_id=1, source_target_pairs={{0,8},{2,10},{8,16},{10,18},{16,24},{18,26},{24,28},{26,30},{28,20... | collective-permute-start | bytes 3244040 | tf_op jit(solution)/shard_map/ppermute | solution.py:151
  59.3 43.3 %collective-permute-start.6 = (bf16[128,4224]{1,0:T(8,128)(2,1)}, bf16[128,4224]{1,0:T(8,128)(2,1)}, u32[]{:S(2)}, u32[]{:S(2)}) collective-permute-start(bf16[128,4224]{1,0:T(8,128)(2,1)} %collective-permute-done.1), channel_id=1, source_target_pairs={{0,4},{2,6},{8,0},{10,2},{16,8},{18,10},{24,16},{26,18},{28,24},{3... | collective-permute-start | bytes 3244040 | tf_op jit(solution)/shard_map/ppermute | solution.py:152
  59.5 14.1 %collective-permute-start.10 = (bf16[1,128,2048]{2,1,0:T(8,128)(2,1)}, bf16[1,128,2048]{2,1,0:T(8,128)(2,1)}, u32[]{:S(2)}, u32[]{:S(2)}) collective-permute-start(bf16[1,128,2048]{2,1,0:T(8,128)(2,1)} %fusion.97), channel_id=1, source_target_pairs={{0,1},{1,0},{2,3},{3,2},{4,5},{5,4},{6,7},{7,6},{8,9},{9,8},{10,11... | collective-permute-start | bytes 1572872 | tf_op jit(solution)/shard_map/ppermute | solution.py:157
  95.0 5.8 %collective-permute-start.9 = (bf16[2,128,2048]{2,1,0:T(8,128)(2,1)S(1)}, bf16[2,128,2048]{2,1,0:T(8,128)(2,1)S(1)}, u32[]{:S(2)}, u32[]{:S(2)}) collective-permute-start(bf16[2,128,2048]{2,1,0:T(8,128)(2,1)S(1)} %slice_bitcast_fusion.12), channel_id=1, source_target_pairs={{0,2},{2,0},{4,6},{6,4},{8,10},{10,8},{12,14},{14,12},{16,18},{18,... | collective-permute-start | bytes 3145736 | tf_op jit(solution)/shard_map/ppermute | solution.py:133
  107.4 31.9 %collective-permute-start.13 = (bf16[256,4224]{1,0:T(8,128)(2,1)}, bf16[256,4224]{1,0:T(8,128)(2,1)}, u32[]{:S(2)}, u32[]{:S(2)}) collective-permute-start(bf16[256,4224]{1,0:T(8,128)(2,1)} %constant_dynamic-update-slice_fusion.7), channel_id=1, source_target_pairs={{0,2},{2,0},{4,6},{6,4},{8,10},{10,8},{12,14},{14,12},{16,18},{18,... | collective-permute-start | bytes 6488072 | tf_op jit(solution)/shard_map/ppermute | solution.py:98
  109.2 57.0 %collective-permute-start.11 = (bf16[128,4224]{1,0:T(8,128)(2,1)}, bf16[128,4224]{1,0:T(8,128)(2,1)}, u32[]{:S(2)}, u32[]{:S(2)}) collective-permute-start(bf16[128,4224]{1,0:T(8,128)(2,1)} %collective-permute-done.5), channel_id=1, source_target_pairs={{0,8},{2,10},{8,16},{10,18},{16,24},{18,26},{24,28},{26,30},{28,20... | collective-permute-start | bytes 3244040 | tf_op jit(solution)/shard_map/ppermute | solution.py:151
  110.9 55.4 %collective-permute-start.12 = (bf16[128,4224]{1,0:T(8,128)(2,1)}, bf16[128,4224]{1,0:T(8,128)(2,1)}, u32[]{:S(2)}, u32[]{:S(2)}) collective-permute-start(bf16[128,4224]{1,0:T(8,128)(2,1)} %collective-permute-done.6), channel_id=1, source_target_pairs={{0,4},{2,6},{8,0},{10,2},{16,8},{18,10},{24,16},{26,18},{28,24},{3... | collective-permute-start | bytes 3244040 | tf_op jit(solution)/shard_map/ppermute | solution.py:152
  111.2 25.3 %collective-permute-start.16 = (bf16[2,128,2048]{2,1,0:T(8,128)(2,1)}, bf16[2,128,2048]{2,1,0:T(8,128)(2,1)}, u32[]{:S(2)}, u32[]{:S(2)}) collective-permute-start(bf16[2,128,2048]{2,1,0:T(8,128)(2,1)} %fusion.12), channel_id=1, source_target_pairs={{0,1},{1,0},{2,3},{3,2},{4,5},{5,4},{6,7},{7,6},{8,9},{9,8},{10,11... | collective-permute-start | bytes 3145736 | tf_op jit(solution)/shard_map/ppermute | solution.py:157
  158.8 6.0 %collective-permute-start.15 = (bf16[2,128,2048]{2,1,0:T(8,128)(2,1)S(1)}, bf16[2,128,2048]{2,1,0:T(8,128)(2,1)S(1)}, u32[]{:S(2)}, u32[]{:S(2)}) collective-permute-start(bf16[2,128,2048]{2,1,0:T(8,128)(2,1)S(1)} %slice_bitcast_fusion.8), channel_id=1, source_target_pairs={{0,2},{2,0},{4,6},{6,4},{8,10},{10,8},{12,14},{14,12},{16,18},{18,... | collective-permute-start | bytes 3145736 | tf_op jit(solution)/shard_map/ppermute | solution.py:133
  170.9 34.6 %collective-permute-start.19 = (bf16[256,4224]{1,0:T(8,128)(2,1)}, bf16[256,4224]{1,0:T(8,128)(2,1)}, u32[]{:S(2)}, u32[]{:S(2)}) collective-permute-start(bf16[256,4224]{1,0:T(8,128)(2,1)} %constant_dynamic-update-slice_fusion.9), channel_id=1, source_target_pairs={{0,2},{2,0},{4,6},{6,4},{8,10},{10,8},{12,14},{14,12},{16,18},{18,... | collective-permute-start | bytes 6488072 | tf_op jit(solution)/shard_map/ppermute | solution.py:98
  175.5 57.1 %collective-permute-start.17 = (bf16[128,2048]{1,0:T(8,128)(2,1)}, bf16[128,2048]{1,0:T(8,128)(2,1)}, u32[]{:S(2)}, u32[]{:S(2)}) collective-permute-start(bf16[128,2048]{1,0:T(8,128)(2,1)} %slice.444), channel_id=1, source_target_pairs={{0,8},{2,10},{8,16},{10,18},{16,24},{18,26},{24,28},{26,30},{28,20... | collective-permute-start | bytes 1572872 | tf_op jit(solution)/shard_map/ppermute | solution.py:154
  177.2 55.5 %collective-permute-start.18 = (bf16[128,2176]{1,0:T(8,128)(2,1)}, bf16[128,2176]{1,0:T(8,128)(2,1)}, u32[]{:S(2)}, u32[]{:S(2)}) collective-permute-start(bf16[128,2176]{1,0:T(8,128)(2,1)} %slice.445), channel_id=1, source_target_pairs={{0,4},{2,6},{8,0},{10,2},{16,8},{18,10},{24,16},{26,18},{28,24},{3... | collective-permute-start | bytes 1671176 | tf_op jit(solution)/shard_map/ppermute | solution.py:155
  177.5 25.3 %collective-permute-start.22 = (bf16[2,128,2048]{2,1,0:T(8,128)(2,1)}, bf16[2,128,2048]{2,1,0:T(8,128)(2,1)}, u32[]{:S(2)}, u32[]{:S(2)}) collective-permute-start(bf16[2,128,2048]{2,1,0:T(8,128)(2,1)} %fusion.10), channel_id=1, source_target_pairs={{0,1},{1,0},{2,3},{3,2},{4,5},{5,4},{6,7},{7,6},{8,9},{9,8},{10,11... | collective-permute-start | bytes 3145736 | tf_op jit(solution)/shard_map/ppermute | solution.py:157
  224.9 6.3 %collective-permute-start.21 = (bf16[2,128,2048]{2,1,0:T(8,128)(2,1)S(1)}, bf16[2,128,2048]{2,1,0:T(8,128)(2,1)S(1)}, u32[]{:S(2)}, u32[]{:S(2)}) collective-permute-start(bf16[2,128,2048]{2,1,0:T(8,128)(2,1)S(1)} %slice_bitcast_fusion.4), channel_id=1, source_target_pairs={{0,2},{2,0},{4,6},{6,4},{8,10},{10,8},{12,14},{14,12},{16,18},{18,... | collective-permute-start | bytes 3145736 | tf_op jit(solution)/shard_map/ppermute | solution.py:133
  236.5 28.6 %collective-permute-start.23 = (bf16[128,4224]{1,0:T(8,128)(2,1)}, bf16[128,4224]{1,0:T(8,128)(2,1)}, u32[]{:S(2)}, u32[]{:S(2)}) collective-permute-start(bf16[128,4224]{1,0:T(8,128)(2,1)} %constant_dynamic-update-slice_fusion.11), channel_id=1, source_target_pairs={{0,2},{2,0},{4,6},{6,4},{8,10},{10,8},{12,14},{14,12},{16,18},{18,... | collective-permute-start | bytes 3244040 | tf_op jit(solution)/shard_map/ppermute | solution.py:98
  236.5 25.9 %collective-permute-start.26 = (bf16[2,128,2048]{2,1,0:T(8,128)(2,1)}, bf16[2,128,2048]{2,1,0:T(8,128)(2,1)}, u32[]{:S(2)}, u32[]{:S(2)}) collective-permute-start(bf16[2,128,2048]{2,1,0:T(8,128)(2,1)} %fusion.8), channel_id=1, source_target_pairs={{0,1},{1,0},{2,3},{3,2},{4,5},{5,4},{6,7},{7,6},{8,9},{9,8},{10,11... | collective-permute-start | bytes 3145736 | tf_op jit(solution)/shard_map/ppermute | solution.py:157
  285.2 33.2 %collective-permute-start.27 = (bf16[1,128,2048]{2,1,0:T(8,128)(2,1)}, bf16[1,128,2048]{2,1,0:T(8,128)(2,1)}, u32[]{:S(2)}, u32[]{:S(2)}) collective-permute-start(bf16[1,128,2048]{2,1,0:T(8,128)(2,1)} %fusion.95), channel_id=1, source_target_pairs={{0,1},{1,0},{2,3},{3,2},{4,5},{5,4},{6,7},{7,6},{8,9},{9,8},{10,11... | collective-permute-start | bytes 1572872 | tf_op jit(solution)/shard_map/ppermute | solution.py:163
  288.3 88.8 %collective-permute-start.36 = (f32[2048,8]{0,1:T(8,128)}, f32[2048,8]{0,1:T(8,128)}, u32[]{:S(2)}, u32[]{:S(2)}) collective-permute-start(f32[2048,8]{0,1:T(8,128)} %constant_dynamic-update-slice_fusion.13), channel_id=1, source_target_pairs={{0,1},{1,0},{2,3},{3,2},{4,5},{5,4},{6,7},{7,6},{8,9},{9,8},{10,11... | collective-permute-start | bytes 196616 | tf_op jit(solution)/shard_map/ppermute | solution.py:184
  290.4 106.2 %collective-permute-start.37 = (bf16[16,48,1152]{2,1,0:T(8,128)(2,1)}, bf16[16,48,1152]{2,1,0:T(8,128)(2,1)}, u32[]{:S(2)}, u32[]{:S(2)}) collective-permute-start(bf16[16,48,1152]{2,1,0:T(8,128)(2,1)} %constant_dynamic-update-slice_fusion.33), channel_id=1, source_target_pairs={{0,16},{2,18},{4,20},{6,22},{8,24},{10,26},{12,28},{14,30},{16,0},... | collective-permute-start | bytes 5308424 | tf_op jit(solution)/shard_map/ppermute | solution.py:190
  319.7 16.9 %collective-permute-start.28 = (bf16[128,1024]{1,0:T(8,128)(2,1)S(1)}, bf16[128,1024]{1,0:T(8,128)(2,1)S(1)}, u32[]{:S(2)}, u32[]{:S(2)}) collective-permute-start(bf16[128,1024]{1,0:T(8,128)(2,1)S(1)} %get-tuple-element.226), channel_id=1, source_target_pairs={{0,8},{2,10},{8,16},{10,18},{16,24},{18,26},{24,28},{26,30},{28,20... | collective-permute-start | bytes 786440 | tf_op jit(solution)/shard_map/ppermute | solution.py:174
  321.3 15.2 %collective-permute-start.32 = (bf16[128,1024]{1,0:T(8,128)(2,1)S(1)}, bf16[128,1024]{1,0:T(8,128)(2,1)S(1)}, u32[]{:S(2)}, u32[]{:S(2)}) collective-permute-start(bf16[128,1024]{1,0:T(8,128)(2,1)S(1)} %get-tuple-element.227), channel_id=1, source_target_pairs={{0,4},{2,6},{8,0},{10,2},{16,8},{18,10},{24,16},{26,18},{28,24},{3... | collective-permute-start | bytes 786440 | tf_op jit(solution)/shard_map/ppermute | solution.py:175
  337.8 51.0 %collective-permute-start.29 = (bf16[128,2048]{1,0:T(8,128)(2,1)}, bf16[128,2048]{1,0:T(8,128)(2,1)}, u32[]{:S(2)}, u32[]{:S(2)}) collective-permute-start(bf16[128,2048]{1,0:T(8,128)(2,1)} %get-tuple-element.222), channel_id=1, source_target_pairs={{0,8},{2,10},{8,16},{10,18},{16,24},{18,26},{24,28},{26,30},{28,20... | collective-permute-start | bytes 1572872 | tf_op jit(solution)/shard_map/ppermute | solution.py:179
  377.1 14.6 %collective-permute-start.33 = (bf16[128,2048]{1,0:T(8,128)(2,1)}, bf16[128,2048]{1,0:T(8,128)(2,1)}, u32[]{:S(2)}, u32[]{:S(2)}) collective-permute-start(bf16[128,2048]{1,0:T(8,128)(2,1)} %get-tuple-element.223), channel_id=1, source_target_pairs={{0,4},{2,6},{8,0},{10,2},{16,8},{18,10},{24,16},{26,18},{28,24},{3... | collective-permute-start | bytes 1572872 | tf_op jit(solution)/shard_map/ppermute | solution.py:180
  394.6 28.0 %collective-permute-start.30 = (bf16[128,2048]{1,0:T(8,128)(2,1)}, bf16[128,2048]{1,0:T(8,128)(2,1)}, u32[]{:S(2)}, u32[]{:S(2)}) collective-permute-start(bf16[128,2048]{1,0:T(8,128)(2,1)} %get-tuple-element.220), channel_id=1, source_target_pairs={{0,8},{2,10},{8,16},{10,18},{16,24},{18,26},{24,28},{26,30},{28,20... | collective-permute-start | bytes 1572872 | tf_op jit(solution)/shard_map/ppermute | solution.py:179
  396.4 26.3 %collective-permute-start.34 = (bf16[128,2048]{1,0:T(8,128)(2,1)}, bf16[128,2048]{1,0:T(8,128)(2,1)}, u32[]{:S(2)}, u32[]{:S(2)}) collective-permute-start(bf16[128,2048]{1,0:T(8,128)(2,1)} %get-tuple-element.221), channel_id=1, source_target_pairs={{0,4},{2,6},{8,0},{10,2},{16,8},{18,10},{24,16},{26,18},{28,24},{3... | collective-permute-start | bytes 1572872 | tf_op jit(solution)/shard_map/ppermute | solution.py:180
  424.4 12.1 %collective-permute-start.35 = (bf16[128,2048]{1,0:T(8,128)(2,1)S(1)}, bf16[128,2048]{1,0:T(8,128)(2,1)S(1)}, u32[]{:S(2)}, u32[]{:S(2)}) collective-permute-start(bf16[128,2048]{1,0:T(8,128)(2,1)S(1)} %get-tuple-element.219), channel_id=1, source_target_pairs={{0,4},{2,6},{8,0},{10,2},{16,8},{18,10},{24,16},{26,18},{28,24},{3... | collective-permute-start | bytes 1572872 | tf_op jit(solution)/shard_map/ppermute | solution.py:180
  424.5 12.0 %collective-permute-start.31 = (bf16[128,2048]{1,0:T(8,128)(2,1)S(1)}, bf16[128,2048]{1,0:T(8,128)(2,1)S(1)}, u32[]{:S(2)}, u32[]{:S(2)}) collective-permute-start(bf16[128,2048]{1,0:T(8,128)(2,1)S(1)} %get-tuple-element.218), channel_id=1, source_target_pairs={{0,8},{2,10},{8,16},{10,18},{16,24},{18,26},{24,28},{26,30},{28,20... | collective-permute-start | bytes 1572872 | tf_op jit(solution)/shard_map/ppermute | solution.py:179
  (83 other events, 651.7 us)
Sparse Core Ops, SparseCore 0:
  379.4 53.6 reduce-scatter.1

commit v3 on v2

--- a/solution.py
+++ b/solution.py
@@ -1,7 +1,11 @@
+import functools
+
 import jax
 import jax.numpy as jnp
 import numpy as np
 from jax import lax
+from jax.experimental import pallas as pl
+from jax.experimental.pallas import tpu as pltpu
 from jax.sharding import PartitionSpec as P
 
 F32 = jnp.float32
@@ -24,13 +28,16 @@
 def block_tables(order):
     chips = len(order)
     half = chips // 2
-    hops = [0] + [hop for step in range(1, half) for hop in (-step, step)] + [half]
+    groups = [[0]] + [[-step, step] for step in range(1, half)] + [[half]]
     ep_count = 2 * chips
     arrival = np.zeros((ep_count, ep_count), np.int32)
     for place, chip in enumerate(order):
         for core in range(2):
             arrival[chip * 2 + core] = [
-                order[(place + hop) % chips] * 2 + (core ^ side) for hop in hops for side in range(2)
+                order[(place + hop) % chips] * 2 + (core ^ side)
+                for hops in groups
+                for side in range(2)
+                for hop in hops
             ]
     spot = np.argsort(arrival, axis=1).astype(np.int32)
     partner = np.arange(ep_count) ^ (ep_count // 2)
@@ -40,6 +47,116 @@
 
 def dot(a, b, ca, cb):
     return lax.dot_general(a, b, (((ca,), (cb,)), ((), ())), preferred_element_type=F32)
+
+
+def group_kernel(pieces, top_k, capacity, share, facts, *refs):
+    x_refs, cot_refs, note_refs = refs[:pieces], refs[pieces : 2 * pieces], refs[2 * pieces : 3 * pieces]
+    gate_ref, up_ref, down_ref = refs[3 * pieces : 3 * pieces + 3]
+    acts, near_other, near_mine, far_other, far_mine, d_weights, packed, out_sum, back_sum = refs[3 * pieces + 3 :]
+    slot, last = pl.program_id(0), pl.num_programs(0) - 1
+    x = jnp.concatenate([ref[...] for ref in x_refs], axis=0)
+    cot = jnp.concatenate([ref[...] for ref in cot_refs], axis=0)
+    said = jnp.concatenate([ref[...] for ref in note_refs], axis=0).astype(F32)
+    tok_count = note_refs[0].shape[0]
+    lanes = said.shape[1]
+    lane = lax.broadcasted_iota(jnp.int32, said.shape, 1)
+    chosen = (said.astype(jnp.int32) == facts[1 + slot]) & (lane < top_k)
+    weight = pltpu.roll(said, lanes - top_k, 1) + (
+        pltpu.roll(said, lanes - 2 * top_k, 1) + pltpu.roll(said, lanes - 3 * top_k, 1)
+    )
+    gain = jnp.sum(jnp.where(chosen, weight, 0.0), axis=1, keepdims=True)
+    w_gate, w_up, w_down = gate_ref[0], up_ref[0], down_ref[0]
+    gate, upper = dot(x, w_gate, 1, 0), dot(x, w_up, 1, 0)
+    pulled = dot(cot, w_down, 1, 1)
+    sigma = jax.nn.sigmoid(gate)
+    active = gate * sigma
+    hidden = active * upper
+    traded = jnp.where(chosen, jnp.sum(hidden * pulled, axis=1, keepdims=True), 0.0)
+    d_hidden = pulled * gain
+    hidden = (hidden * gain).astype(BF16)
+    d_gate = (d_hidden * upper * sigma * (1.0 + gate * (1.0 - sigma))).astype(BF16)
+    d_up = (d_hidden * active).astype(BF16)
+    act = jnp.concatenate([hidden, d_gate, d_up], axis=1)
+    acts[0] = act
+    out = dot(hidden, w_down, 1, 0)
+    back = dot(d_gate, w_gate, 1, 1) + dot(d_up, w_up, 1, 1)
+
+    @pl.when(slot == 0)
+    def _():
+        out_sum[...] = out
+        back_sum[...] = back
+        d_weights[...] = traded
+
+    @pl.when(slot > 0)
+    def _():
+        out_sum[...] += out
+        back_sum[...] += back
+        d_weights[...] += traded
+
+    @pl.when(slot == last)
+    def _():
+        near = pieces // 2 * tok_count
+        for value, at in ((out_sum, 0), (back_sum, share)):
+            low, high = value[:, :share].astype(BF16), value[:, share:].astype(BF16)
+            mine = jnp.where(facts[0] == 0, low, high)
+            other = jnp.where(facts[0] == 0, high, low)
+            near_other[:, at : at + share] = other[:near]
+            near_mine[:, at : at + share] = mine[:near]
+            far_other[:, at : at + share] = other[near:]
+            far_mine[:, at : at + share] = mine[near:]
+        named = jnp.max(jnp.where(chosen, 1.0, 0.0), axis=1, keepdims=True)
+        row = lax.broadcasted_iota(jnp.int32, (tok_count, tok_count), 0)
+        column = lax.broadcasted_iota(jnp.int32, (tok_count, tok_count), 1)
+        earlier = jnp.where(column < row, 1.0, 0.0).astype(BF16)
+        for piece in range(pieces):
+            rows = slice(piece * tok_count, (piece + 1) * tok_count)
+            mask = jnp.broadcast_to(named[rows], (tok_count, tok_count))
+            position = dot(earlier, mask.astype(BF16), 1, 0).astype(jnp.int32)
+            pick = jnp.where((position == column) & (mask > 0.0), 1.0, 0.0).astype(BF16)
+            packed[piece] = dot(pick, act[rows], 0, 0).astype(BF16)[:capacity]
+
+
+def group_call(x_pieces, cot_pieces, note_pieces, facts, weights, top_k, capacity, share):
+    pieces = len(x_pieces)
+    gate_w, up_w, down_w = weights
+    per_device, width, units = gate_w.shape
+    tok_count = x_pieces[0][0].shape[0]
+    rows = pieces * tok_count
+    lanes = 128
+
+    def columns(piece, size):
+        return pl.BlockSpec((tok_count, size), lambda slot, at=piece[1]: (0, at))
+
+    half = rows // 2
+    wide = jax.ShapeDtypeStruct((half, 2 * share), BF16)
+    whole = pl.BlockSpec((half, 2 * share), lambda slot: (0, 0))
+    return pl.pallas_call(
+        functools.partial(group_kernel, pieces, top_k, capacity, share),
+        grid=(per_device,),
+        in_specs=[pl.BlockSpec(memory_space=pltpu.SMEM)]
+        + [columns(piece, width) for piece in x_pieces + cot_pieces]
+        + [columns(piece, lanes) for piece in note_pieces]
+        + [pl.BlockSpec((1,) + w.shape[1:], lambda slot: (slot, 0, 0)) for w in weights],
+        out_specs=[pl.BlockSpec((1, rows, 3 * units), lambda slot: (slot, 0, 0))]
+        + [whole] * 4
+        + [
+            pl.BlockSpec((rows, lanes), lambda slot: (0, 0)),
+            pl.BlockSpec((pieces, capacity, 3 * units), lambda slot: (0, 0, 0)),
+        ],
+        out_shape=[jax.ShapeDtypeStruct((per_device, rows, 3 * units), BF16)]
+        + [wide] * 4
+        + [
+            jax.ShapeDtypeStruct((rows, lanes), F32),
+            jax.ShapeDtypeStruct((pieces, capacity, 3 * units), BF16),
+        ],
+        scratch_shapes=[pltpu.VMEM((rows, width), F32)] * 2,
+        compiler_params=pltpu.CompilerParams(vmem_limit_bytes=60 * 1024 * 1024),
+        cost_estimate=pl.CostEstimate(
+            flops=12 * rows * width * units * per_device,
+            bytes_accessed=12 * width * units * per_device // 2 + 12 * rows * width,
+            transcendentals=rows * units * per_device,
+        ),
+    )(facts, *[p[0] for p in x_pieces], *[p[0] for p in cot_pieces], *[p[0] for p in note_pieces], *weights)
 
 
 def gather_body(tokens, expert_ids, combine, cotangent, old_layout, pair_moves, gate_w, up_w, down_w):
@@ -74,101 +191,76 @@
         wanted = jnp.arange(capacity, dtype=jnp.int32)[None, :, None]
         return ((position[:, None, :] == wanted) & named[:, None, :]).astype(BF16)
 
-    both = per_device * units
-    w_in = jnp.concatenate([gate_w[l] for l in range(per_device)] + [up_w[l] for l in range(per_device)], axis=1)
-    w_out = down_w.reshape(both, width)
-    mine_at, other_at = my_share * share, (1 - my_share) * share
-    w_in_mine = lax.dynamic_slice_in_dim(w_in, mine_at, share, 0)
-    w_in_other = lax.dynamic_slice_in_dim(w_in, other_at, share, 0)
-    w_out_mine = lax.dynamic_slice_in_dim(w_out, mine_at, share, 1)
-    w_out_other = lax.dynamic_slice_in_dim(w_out, other_at, share, 1)
-
-    parts = []
+    facts = jnp.concatenate([my_share[None], experts]).astype(jnp.int32)
+
+    parts = [expert_ids.astype(F32)]
     rest = combine
     for _ in range(3):
         parts.append(lax.reduce_precision(rest, 8, 7))
         rest = rest - parts[-1]
-    id_parts = [expert_ids // 256, expert_ids % 256]
-    notes = jnp.concatenate([part.astype(BF16) for part in id_parts + parts], axis=1)
-    notes = jnp.pad(notes, ((0, 0), (0, -notes.shape[1] % 128)))
+    notes = jnp.concatenate(parts, axis=1)
+    notes = jnp.pad(notes, ((0, 0), (0, -notes.shape[1] % 128))).astype(BF16)
     payload = jnp.concatenate([tokens, cotangent, notes], axis=1)
-
-    def compute(pieces):
-        near = jnp.concatenate(pieces)
-        far = lax.ppermute(near, "ep", other_core)
-        count = len(pieces)
-        near, far = near.reshape(count, tok_count, -1), far.reshape(count, tok_count, -1)
-        group = jnp.stack([near, far], axis=1).reshape(count * 2 * tok_count, -1)
-        x, cot, said = group[:, :width], group[:, width : 2 * width], group[:, 2 * width :].astype(F32)
-        columns = [said[:, i * top_k : (i + 1) * top_k] for i in range(5)]
-        ids = (columns[0] * 256 + columns[1]).astype(jnp.int32)
-        weights = columns[2] + (columns[3] + columns[4])
-        gains = [
-            jnp.sum(jnp.where(ids == experts[l], weights, 0.0), axis=1, keepdims=True) for l in range(per_device)
-        ]
-        gains_wide = jnp.concatenate([jnp.broadcast_to(gain, (gain.shape[0], units)) for gain in gains], axis=1)
-        projected = dot(x, w_in, 1, 0)
-        pulled = dot(cot, w_out, 1, 1)
-        gate, upper = projected[:, :both], projected[:, both:]
-        sigma = jax.nn.sigmoid(gate)
-        active = gate * sigma
-        hidden = active * upper
-        traded = hidden * pulled
-        d_weights = sum(
-            jnp.where(
-                ids == experts[l], jnp.sum(traded[:, l * units : (l + 1) * units], axis=1, keepdims=True), 0.0
-            )
-            for l in range(per_device)
-        )
-        d_hidden = pulled * gains_wide
-        hidden = (hidden * gains_wide).astype(BF16)
-        d_gate = (d_hidden * upper * sigma * (1.0 + gate * (1.0 - sigma))).astype(BF16)
-        d_up = (d_hidden * active).astype(BF16)
-        d_in = jnp.concatenate([d_gate, d_up], axis=1)
-
-        def partial_sum(w_o, w_i):
-            out = dot(hidden, w_o, 1, 0).astype(BF16)
-            back = dot(d_in, w_i, 1, 1).astype(BF16)
-            value = jnp.concatenate([out, back], axis=1).reshape(count, 2, tok_count, 2 * share)
-            arrived = lax.ppermute(value[:, 1], "ep", other_core)
-            return value[:, 0].astype(F32) + arrived.astype(F32)
-
-        sent = partial_sum(w_out_other, w_in_other).astype(BF16)
-        kept = partial_sum(w_out_mine, w_in_mine).astype(BF16)
-        ids = ids.reshape(2 * count, tok_count, top_k)
-        tail = slice(last * units, (last + 1) * units)
-        packed = jnp.concatenate([hidden[:, tail], d_gate[:, tail], d_up[:, tail]], axis=1)
-        packed = packed.reshape(2 * count, tok_count, 3 * units)
-        packed = jnp.einsum("brt,btf->brf", rows_of(experts[last], ids), packed, preferred_element_type=F32)
-        return (x, cot, hidden, d_gate, d_up, d_weights, ids, packed.astype(BF16)), sent, kept
+    note_at = 2 * width // notes.shape[1]
+
+    def add_pair(a, b):
+        return (a.astype(F32) + b.astype(F32)).astype(BF16)
+
+    def whole(piece):
+        return ((piece, 0), (piece, 1), (piece, note_at))
+
+    def halves(first, second):
+        return ((first, 0), (second, 0), (second, width // notes.shape[1]))
 
     kept_groups, totals = [], []
     right = left = payload
-    pending = None
+    pending = crossing = None
     for step in range(half + 1):
-        pieces = [payload] if step == 0 else [right, left] if step < half else [jnp.concatenate([right, left], axis=1)]
+        near = [payload] if step == 0 else [right, left]
+        far = [lax.ppermute(piece, "ep", other_core) for piece in near]
+        if step == half:
+            pieces = [halves(*near), halves(*far)]
+        else:
+            pieces = [whole(piece) for piece in near + far]
         if step < half - 1:
             right = lax.ppermute(right, "ep", forward)
             left = lax.ppermute(left, "ep", backward)
         elif step == half - 1:
             right = lax.ppermute(right[:, :width], "ep", forward)
             left = lax.ppermute(left[:, width:], "ep", backward)
+        if crossing is not None:
+            totals.append(add_pair(*crossing))
+            crossing = None
         if pending is not None:
-            arrived = lax.ppermute(pending[0], "tp", other_share)
-            totals.append((pending[1].astype(F32) + arrived.astype(F32)).astype(BF16))
-        group, sent, kept = compute(pieces)
-        right, left, sent, kept, group, totals = lax.optimization_barrier((right, left, sent, kept, group, totals))
-        kept_groups.append(group)
-        pending = (sent, kept)
-    arrived = lax.ppermute(pending[0], "tp", other_share)
-    totals.append((pending[1].astype(F32) + arrived.astype(F32)).astype(BF16))
-
-    x, cot, hidden, d_gate, d_up, d_weights, ids, packed = (
-        jnp.concatenate([group[i] for group in kept_groups], axis=0) for i in range(8)
-    )
-    by_hop = {0: totals[0][0], half: totals[half][0]}
+            near_other, near_mine, far_other, far_mine = pending
+            sent = add_pair(near_other, lax.ppermute(far_other, "ep", other_core))
+            kept = add_pair(near_mine, lax.ppermute(far_mine, "ep", other_core))
+            crossing = (kept, lax.ppermute(sent, "tp", other_share))
+        acts, *pending, d_part, packed = group_call(
+            *[list(part) for part in zip(*pieces)], facts, (gate_w, up_w, down_w), top_k, capacity, share
+        )
+        group = (acts, d_part, packed)
+        right, left, pending, crossing, group, totals = lax.optimization_barrier(
+            (right, left, pending, crossing, group, totals)
+        )
+        kept_groups.append((pieces, *group))
+    totals.append(add_pair(*crossing))
+    near_other, near_mine, far_other, far_mine = pending
+    sent = add_pair(near_other, lax.ppermute(far_other, "ep", other_core))
+    kept = add_pair(near_mine, lax.ppermute(far_mine, "ep", other_core))
+    totals.append(add_pair(kept, lax.ppermute(sent, "tp", other_share)))
+
+    every = [piece for group in kept_groups for piece in group[0]]
+    x = jnp.concatenate([array[:, at * width : (at + 1) * width] for (array, at), _, _ in every])
+    cot = jnp.concatenate([array[:, at * width : (at + 1) * width] for _, (array, at), _ in every])
+    ids = jnp.concatenate([array[:, at * 128 : at * 128 + top_k] for _, _, (array, at) in every])
+    ids = ids.astype(jnp.int32).reshape(ep_count, tok_count, top_k)
+    acts = jnp.concatenate([group[1] for group in kept_groups], axis=1)
+    d_weights = jnp.concatenate([group[2] for group in kept_groups])[:, :top_k]
+    packed = jnp.concatenate([group[3] for group in kept_groups])
+    by_hop = {0: totals[0], half: totals[half]}
     for step in range(1, half):
-        by_hop[-step], by_hop[step] = totals[step][0], totals[step][1]
+        by_hop[-step], by_hop[step] = totals[step][:tok_count], totals[step][tok_count:]
 
     up_sum, down_sum = by_hop[half][:, :share], by_hop[half][:, share:]
     up_sum = jnp.pad(lax.ppermute(up_sum, "ep", forward).astype(F32), ((0, 0), (0, share)))
@@ -192,13 +284,14 @@
     spread_rows = jnp.einsum("brt,brf->btf", rows_of(new_last, ids), packed, preferred_element_type=F32).astype(BF16)
     spread_rows = spread_rows.reshape(ep_count * tok_count, 3 * units)
 
-    def grads(left_side, own, moved):
-        parts = [left_side(own[:, l * units : (l + 1) * units]) for l in range(last)] + [left_side(moved)]
-        return jnp.stack(parts)
-
-    grad_gate = grads(lambda v: dot(x, v, 0, 0).astype(BF16), d_gate, spread_rows[:, units : 2 * units])
-    grad_up = grads(lambda v: dot(x, v, 0, 0).astype(BF16), d_up, spread_rows[:, 2 * units :])
-    grad_down = grads(lambda v: dot(v, cot, 0, 0).astype(BF16), hidden, spread_rows[:, :units])
+    def grads(multiply, at):
+        columns = slice(at * units, (at + 1) * units)
+        own = [multiply(acts[l, :, columns]) for l in range(last)]
+        return jnp.stack(own + [multiply(spread_rows[:, columns])])
+
+    grad_down = grads(lambda v: dot(v, cot, 0, 0).astype(BF16), 0)
+    grad_gate = grads(lambda v: dot(x, v, 0, 0).astype(BF16), 1)
+    grad_up = grads(lambda v: dot(x, v, 0, 0).astype(BF16), 2)
     return (mixed, d_tokens, d_combine, grad_gate, grad_up, grad_down)
 
 
@@ -319,7 +412,8 @@
     tok_count, top_k = expert_ids.shape
     ep_count = lax.axis_size("ep")
     rows = 3 * tok_count * top_k * ep_count // (2 * old_layout.shape[0]) * operands[6].shape[0]
-    return (gather_body if ep_count * tok_count <= 2 * rows else dispatch_body)(*operands)
+    gather = ep_count * tok_count <= 2 * rows and old_layout.shape[0] <= 256
+    return (gather_body if gather else dispatch_body)(*operands)
 
 
 def solution(mesh):

time: 453 us -> 423 us (0.934)
  Pallas kernels: 0 us -> 101 us
  matrix products: 95.4 us -> 43.9 us
  other arithmetic: 86.3 us -> 48.8 us
  local copies, waits for them, and re-layouts: 102 us -> 78.9 us
  waiting for transfers between devices: 73.9 us -> 54.9 us
    pallas_call x0 -> x5, Pallas kernels: none -> 101 us  [group_call(): pl.pallas_call(functools.partial(group_kernel, pieces, top_k, capacity, s...]
    dot_general x36 -> x6, matrix products: 85.7 us -> 42.3 us  [dot(): lax.dot_general(a, b, (((ca,), (cb,)), ((), ())), preferred_element_type=...]
    another operation x9 -> x4, other arithmetic: 21.4 us -> 6.66 us  [the longest x3 5.97 us: grads(): return jnp.stack(own + [multiply(spread_rows[:, columns])])]
    ppermute x20 -> x24, waiting for transfers between devices: 40.8 us -> 26.6 us  [the longest x4 21.1 us: gather_body(): crossing = (kept, lax.ppermute(sent, 'tp', other_share))]
    concatenate x12 -> x7, local copies, waits for them, and re-layouts: 14.4 us -> 4.77 us  [the longest x1 1.91 us: gather_body(): jnp.concatenate([array[:, at * width:(at + 1) * width] for (array, at), _...]
    optimization_barrier x10 -> x0, local copies, waits for them, and re-layouts: 7.86 us -> none  [gather_body(): lax.optimization_barrier((right, left, sent, kept, group, totals))]
    squeeze x11 -> x0, local copies, waits for them, and re-layouts: 5.32 us -> none  [the longest x1 4.74 us: gather_body(): up_w[l]]
    dot_general x5 -> x0, matrix products: 5.23 us -> none  [compute(): jnp.einsum('brt,btf->brf', rows_of(experts[last], ids), packed, preferred...]
  transfers between devices with their start and end apart: 39 -> 43, of which waited for: 9 -> 7; matrix products, arithmetic and copies ran while one was open for 54% -> 36% of each run, Pallas kernels for 0% -> 24%
where the time goes in v3:
time: 423 us; the launch traced here: 416 us
  Pallas kernels  101 us (24%)
  local copies, waits for them, and re-layouts  78.9 us (19%)
  starting transfers between devices  70.9 us (17%)
  waiting for transfers between devices  54.9 us (13%)
  other arithmetic  48.8 us (12%)
  matrix products  43.9 us (10%)
  between operations  16.9 us (4%)
    pallas_call x5, Pallas kernels, group_call(): pl.pallas_call(functools.partial(group_kernel, pieces, top_k, capacity, s...  101 us
    unnamed x124, local copies, waits for them, and re-layouts  50.5 us
    ppermute x3, starting transfers between devices, gather_body(): up_sum = lax.ppermute(up_sum, 'ep', forward).astype(F32)  46 us
    dot_general x6, matrix products, dot(): lax.dot_general(a, b, (((ca,), (cb,)), ((), ())), preferred_element_type=...  42.3 us
    convert_element_type x14, other arithmetic, add_pair(): return (a.astype(F32) + b.astype(F32)).astype(BF16)  29.6 us
    ppermute x4, waiting for transfers between devices, gather_body(): crossing = (kept, lax.ppermute(sent, 'tp', other_share))  21.1 us
    ppermute x1, waiting for transfers between devices, gather_body(): lax.ppermute(up_sum, 'ep', forward).astype(F32)  12.3 us
    ppermute x3, waiting for transfers between devices, gather_body(): down_sum = lax.ppermute(down_sum, 'ep', backward).astype(F32)  10.9 us
  transfers between devices with their start and end apart: 43, of which 7 were waited for; matrix products, arithmetic and copies ran while one was open for 36% of the time, Pallas kernels for 24%

profile of v3, /device:TPU:0, one launch (start us, length us, event | category | flops | bytes accessed | tf_op | source)
XLA Modules:
  0.0 415.5 jit_solution(3865084246845705077)
XLA Ops:
  11.4 2.6 collective-permute-start
  25.5 14.1 %shard_map.154 = (bf16[2,256,1152]{2,1,0:T(8,128)(2,1)}, bf16[128,2048]{1,0:T(8,128)(2,1)}, bf16[128,2048]{1,0:T(8,128)(2,1)}, bf16[128,2048]{1,0:T(8,128)(2,1)}...) custom-call(s32[3]{0:T(128)} %pad_add_fusion.facts, ...), custom_call_target="tpu_custom_call" | custom-call | flops 4831838208 | bytes 15728640 | tf_op jit(solution)/shard_map/pallas_call | solution.py:133
  46.1 2.4 constant_dynamic-update-slice_fusion.13
  59.3 24.2 %shard_map.155 = (bf16[2,512,1152]{2,1,0:T(8,128)(2,1)}, bf16[256,2048]{1,0:T(8,128)(2,1)}, bf16[256,2048]{1,0:T(8,128)(2,1)}, bf16[256,2048]{1,0:T(8,128)(2,1)}...) custom-call(s32[3]{0:T(128)} %pad_add_fusion.facts, bf16[128,4224]{1,0:T(8,128)(2,1)} %copy-done.12, ...), custom_call_target="tpu_custom_call" | custom-call | flops 9663676416 | bytes 22020096 | tf_op jit(solution)/shard_map/pallas_call | solution.py:133
  107.1 2.6 add_convert_fusion.8
  116.0 24.2 %shard_map.156 = (bf16[2,512,1152]{2,1,0:T(8,128)(2,1)}, bf16[256,2048]{1,0:T(8,128)(2,1)}, bf16[256,2048]{1,0:T(8,128)(2,1)}, bf16[256,2048]{1,0:T(8,128)(2,1)}...) custom-call(s32[3]{0:T(128)} %pad_add_fusion.facts, ...), custom_call_target="tpu_custom_call" | custom-call | flops 9663676416 | bytes 22020096 | tf_op jit(solution)/shard_map/pallas_call | solution.py:133
  140.4 3.0 slice_dynamic-update-slice_fusion.17
  151.9 3.5 constant_dynamic-update-slice_fusion.11
  157.2 2.6 add_convert_fusion.5
  161.4 2.6 add_convert_fusion.6
  165.6 24.3 %shard_map.157 = (bf16[2,512,1152]{2,1,0:T(8,128)(2,1)}, bf16[256,2048]{1,0:T(8,128)(2,1)}, bf16[256,2048]{1,0:T(8,128)(2,1)}, bf16[256,2048]{1,0:T(8,128)(2,1)}...) custom-call(s32[3]{0:T(128)} %pad_add_fusion.facts, ...), custom_call_target="tpu_custom_call" | custom-call | flops 9663676416 | bytes 22020096 | tf_op jit(solution)/shard_map/pallas_call | solution.py:133
  192.3 2.4 slice_dynamic-update-slice_fusion.1
  196.7 2.6 add_convert_fusion.1
  207.5 14.4 %shard_map.158 = (bf16[2,256,1152]{2,1,0:T(8,128)(2,1)}, bf16[128,2048]{1,0:T(8,128)(2,1)}, bf16[128,2048]{1,0:T(8,128)(2,1)}, bf16[128,2048]{1,0:T(8,128)(2,1)}...) custom-call(s32[3]{0:T(128)} %pad_add_fusion.facts, ...), custom_call_target="tpu_custom_call" | custom-call | flops 4831838208 | bytes 15728640 | tf_op jit(solution)/shard_map/pallas_call | solution.py:133
  225.7 2.6 add_convert_fusion.3
  228.3 21.1 %collective-permute-done.28 = bf16[256,2048]{1,0:T(8,128)(2,1)} collective-permute-done((bf16[256,2048]{1,0:T(8,128)(2,1)S(1)}, bf16[256,2048]{1,0:T(8,128)(2,1)}, u32[]{:S(2)}, u32[]{:S(2)}) %collective-permute-start.28) | collective-permute-done | bytes 1048608 | tf_op jit(solution)/shard_map/ppermute | solution.py:238
  250.6 10.0 %fusion = bf16[1,2048,384]{2,1,0:T(8,128)(2,1)} fusion(bf16[2048,2048]{1,0:T(8,128)(2,1)} %constant_dynamic-update-slice_fusion.5, bf16[2,2048,1152]{2,1,0:T(8,128)(2,1)} %constant_dynamic-update-slice_fusion.9), kind=kOutput, calls=%fused_computation.12 | convolution fusion | flops 3222011904 | bytes 11534336 | tf_op jit(solution)/shard_map/dot_general | solution.py:49
  260.6 7.3 %fusion.2 = bf16[1,2048,384]{2,1,0:T(8,128)(2,1)} fusion(bf16[2048,2048]{1,0:T(8,128)(2,1)S(1)} %bitcast.59, bf16[2,2048,1152]{2,1,0:T(8,128)(2,1)} %constant_dynamic-update-slice_fusion.9), kind=kOutput, calls=%fused_computation.14 | convolution fusion | flops 3222011904 | bytes 11534336 | tf_op jit(solution)/shard_map/dot_general | solution.py:49
  270.1 2.6 collective-permute-start.41
  272.7 8.6 %fusion.4 = bf16[1,384,2048]{2,1,0:T(8,128)(2,1)} fusion(bf16[2048,2048]{1,0:T(8,128)(2,1)} %slice_dynamic-update-slice_fusion, bf16[2,2048,1152]{2,1,0:T(8,128)(2,1)} %constant_dynamic-update-slice_fusion.9), kind=kOutput, calls=%fused_computation.16 | convolution fusion | flops 3222011904 | bytes 11534336 | tf_op jit(solution)/shard_map/dot_general | solution.py:49
  281.3 2.6 add_convert_fusion
  290.0 2.9 gather_fusion
  294.4 5.4 %collective-permute-done.31 = bf16[128,2048]{1,0:T(8,128)(2,1)} collective-permute-done((bf16[128,2048]{1,0:T(8,128)(2,1)}, bf16[128,2048]{1,0:T(8,128)(2,1)}, u32[]{:S(2)}, u32[]{:S(2)}) %collective-permute-start.31) | collective-permute-done | bytes 524320 | tf_op jit(solution)/shard_map/ppermute | solution.py:251
  304.1 12.3 %collective-permute-done.32 = bf16[128,1024]{1,0:T(8,128)(2,1)S(1)} collective-permute-done((bf16[128,1024]{1,0:T(8,128)(2,1)S(1)}, bf16[128,1024]{1,0:T(8,128)(2,1)S(1)}, u32[]{:S(2)}, u32[]{:S(2)}) %collective-permute-start.32) | collective-permute-done | bytes 262176 | tf_op jit(solution)/shard_map/ppermute | solution.py:266
  317.4 39.8 %collective-permute-start.33 = (bf16[128,2048]{1,0:T(8,128)(2,1)}, bf16[128,2048]{1,0:T(8,128)(2,1)}, u32[]{:S(2)}, u32[]{:S(2)}) collective-permute-start(bf16[128,2048]{1,0:T(8,128)(2,1)} %get-tuple-element.223), channel_id=1, source_target_pairs={{0,8},{2,10},{8,16},{10,18},{16,24},{18,26},{24,28},{26,30},{28,20... | collective-permute-start | bytes 1572872 | tf_op jit(solution)/shard_map/ppermute | solution.py:271
  361.0 8.1 %fusion.1 = bf16[1,2048,384]{2,1,0:T(8,128)(2,1)S(1)} fusion(bf16[2048,2048]{1,0:T(8,128)(2,1)} %constant_dynamic-update-slice_fusion.5, bf16[2048,1152]{1,0:T(8,128)(2,1)S(1)} %bitcast.54), kind=kOutput, calls=%fused_computation.13 | convolution fusion | flops 3222011904 | bytes 11534336 | tf_op jit(solution)/shard_map/dot_general | solution.py:49
  369.2 4.7 %fusion.3 = bf16[1,2048,384]{2,1,0:T(8,128)(2,1)S(1)} fusion(bf16[2048,2048]{1,0:T(8,128)(2,1)S(1)} %bitcast.61, bf16[2048,1152]{1,0:T(8,128)(2,1)S(1)} %bitcast.55), kind=kOutput, calls=%fused_computation.15 | convolution fusion | flops 3222011904 | bytes 11534336 | tf_op jit(solution)/shard_map/dot_general | solution.py:49
  375.5 4.2 %collective-permute-start.34 = (bf16[128,2048]{1,0:T(8,128)(2,1)S(1)}, bf16[128,2048]{1,0:T(8,128)(2,1)S(1)}, u32[]{:S(2)}, u32[]{:S(2)}) collective-permute-start(bf16[128,2048]{1,0:T(8,128)(2,1)S(1)} %get-tuple-element.221), channel_id=1, source_target_pairs={{0,8},{2,10},{8,16},{10,18},{16,24},{18,26},{24,28},{26,30},{28,20... | collective-permute-start | bytes 1572872 | tf_op jit(solution)/shard_map/ppermute | solution.py:271
  379.9 3.6 fusion.5
  385.6 4.5 %collective-permute-done.34 = bf16[128,2048]{1,0:T(8,128)(2,1)S(1)} collective-permute-done((bf16[128,2048]{1,0:T(8,128)(2,1)S(1)}, bf16[128,2048]{1,0:T(8,128)(2,1)S(1)}, u32[]{:S(2)}, u32[]{:S(2)}) %collective-permute-start.34) | collective-permute-done | bytes 524320 | tf_op jit(solution)/shard_map/ppermute | solution.py:271
  390.1 3.1 collective-permute-done.38
  399.6 7.8 %collective-permute-done.39 = bf16[128,2048]{1,0:T(8,128)(2,1)S(1)} collective-permute-done((bf16[128,2048]{1,0:T(8,128)(2,1)S(1)}, bf16[128,2048]{1,0:T(8,128)(2,1)S(1)}, u32[]{:S(2)}, u32[]{:S(2)}) %collective-permute-start.39) | collective-permute-done | bytes 524320 | tf_op jit(solution)/shard_map/ppermute | solution.py:272
  (280 shorter events, 121.8 us)
Async XLA Ops:
  7.2 401.3 %reduce-scatter.2.cloned.1.call-start = ((), (), s32[]{:S(2)}) async-start(), calls=%async_computation.1 | async-start | bytes 69632 | tf_op jit(solution)/shard_map/reduce_scatter | solution.py:278
  11.0 14.5 %collective-permute-start.2 = (bf16[128,4224]{1,0:T(8,128)(2,1)}, bf16[128,4224]{1,0:T(8,128)(2,1)}, u32[]{:S(2)}, u32[]{:S(2)}) collective-permute-start(bf16[128,4224]{1,0:T(8,128)(2,1)} %fusion.14.refs_0_.refs_2_.refs_4_), channel_id=1, source_target_pairs={{0,2},{2,0},{4,6},{6,4},{8,10},{10,8},{12,14},{14,12},{16,18},{18,... | collective-permute-start | bytes 3244040 | tf_op jit(solution)/shard_map/ppermute | solution.py:220
  11.4 28.2 %collective-permute-start = (bf16[128,4224]{1,0:T(8,128)(2,1)}, bf16[128,4224]{1,0:T(8,128)(2,1)S(1)}, u32[]{:S(2)}, u32[]{:S(2)}) collective-permute-start(bf16[128,4224]{1,0:T(8,128)(2,1)} %fusion.14.refs_0_.refs_2_.refs_4_), channel_id=1, source_target_pairs={{0,8},{2,10},{8,16},{10,18},{16,24},{18,26},{24,28},{26,30},{28,20... | collective-permute-start | bytes 3244040 | tf_op jit(solution)/shard_map/ppermute | solution.py:226
  14.0 26.2 %collective-permute-start.1 = (bf16[128,4224]{1,0:T(8,128)(2,1)}, bf16[128,4224]{1,0:T(8,128)(2,1)S(1)}, u32[]{:S(2)}, u32[]{:S(2)}) collective-permute-start(bf16[128,4224]{1,0:T(8,128)(2,1)} %fusion.14.refs_0_.refs_2_.refs_4_), channel_id=1, source_target_pairs={{0,4},{2,6},{8,0},{10,2},{16,8},{18,10},{24,16},{26,18},{28,24},{3... | collective-permute-start | bytes 3244040 | tf_op jit(solution)/shard_map/ppermute | solution.py:227
  40.2 19.1 %collective-permute-start.5 = (bf16[128,4224]{1,0:T(8,128)(2,1)S(1)}, bf16[128,4224]{1,0:T(8,128)(2,1)}, u32[]{:S(2)}, u32[]{:S(2)}) collective-permute-start(bf16[128,4224]{1,0:T(8,128)(2,1)S(1)} %collective-permute-done.refs_0_.refs_4_.refs_8_), channel_id=1, source_target_pairs={{0,2},{2,0},{4,6},{6,4},{8,10},{10,8},{12,14},{14,12},{16,18},{18,... | collective-permute-start | bytes 3244040 | tf_op jit(solution)/shard_map/ppermute | solution.py:220
  40.2 43.3 %collective-permute-start.3 = (bf16[128,4224]{1,0:T(8,128)(2,1)S(1)}, bf16[128,4224]{1,0:T(8,128)(2,1)}, u32[]{:S(2)}, u32[]{:S(2)}) collective-permute-start(bf16[128,4224]{1,0:T(8,128)(2,1)S(1)} %collective-permute-done.refs_0_.refs_4_.refs_8_), channel_id=1, source_target_pairs={{0,8},{2,10},{8,16},{10,18},{16,24},{18,26},{24,28},{26,30},{28,20... | collective-permute-start | bytes 3244040 | tf_op jit(solution)/shard_map/ppermute | solution.py:226
  41.9 17.5 %collective-permute-start.6 = (bf16[128,4224]{1,0:T(8,128)(2,1)S(1)}, bf16[128,4224]{1,0:T(8,128)(2,1)}, u32[]{:S(2)}, u32[]{:S(2)}) collective-permute-start(bf16[128,4224]{1,0:T(8,128)(2,1)S(1)} %collective-permute-done.1.refs_1_.refs_5_.refs_9_), channel_id=1, source_target_pairs={{0,2},{2,0},{4,6},{6,4},{8,10},{10,8},{12,14},{14,12},{16,18},{18,... | collective-permute-start | bytes 3244040 | tf_op jit(solution)/shard_map/ppermute | solution.py:220
  53.1 30.4 %collective-permute-start.4 = (bf16[128,4224]{1,0:T(8,128)(2,1)S(1)}, bf16[128,4224]{1,0:T(8,128)(2,1)}, u32[]{:S(2)}, u32[]{:S(2)}) collective-permute-start(bf16[128,4224]{1,0:T(8,128)(2,1)S(1)} %collective-permute-done.1.refs_1_.refs_5_.refs_9_), channel_id=1, source_target_pairs={{0,4},{2,6},{8,0},{10,2},{16,8},{18,10},{24,16},{26,18},{28,24},{3... | collective-permute-start | bytes 3244040 | tf_op jit(solution)/shard_map/ppermute | solution.py:227
  55.9 27.7 %collective-permute-start.9 = (bf16[128,2048]{1,0:T(8,128)(2,1)}, bf16[128,2048]{1,0:T(8,128)(2,1)S(1)}, u32[]{:S(2)}, u32[]{:S(2)}) collective-permute-start(bf16[128,2048]{1,0:T(8,128)(2,1)} %add_convert_fusion.20), channel_id=1, source_target_pairs={{0,1},{1,0},{2,3},{3,2},{4,5},{5,4},{6,7},{7,6},{8,9},{9,8},{10,11... | collective-permute-start | bytes 1572872 | tf_op jit(solution)/shard_map/ppermute | solution.py:238
  84.3 25.4 %collective-permute-start.12 = (bf16[128,4224]{1,0:T(8,128)(2,1)}, bf16[128,4224]{1,0:T(8,128)(2,1)}, u32[]{:S(2)}, u32[]{:S(2)}) collective-permute-start(bf16[128,4224]{1,0:T(8,128)(2,1)} %collective-permute-done.3.refs_0_.refs_4_.refs_8_), channel_id=1, source_target_pairs={{0,2},{2,0},{4,6},{6,4},{8,10},{10,8},{12,14},{14,12},{16,18},{18,... | collective-permute-start | bytes 3244040 | tf_op jit(solution)/shard_map/ppermute | solution.py:220
  84.3 55.9 %collective-permute-start.10 = (bf16[128,4224]{1,0:T(8,128)(2,1)}, bf16[128,4224]{1,0:T(8,128)(2,1)}, u32[]{:S(2)}, u32[]{:S(2)}) collective-permute-start(bf16[128,4224]{1,0:T(8,128)(2,1)} %collective-permute-done.3.refs_0_.refs_4_.refs_8_), channel_id=1, source_target_pairs={{0,8},{2,10},{8,16},{10,18},{16,24},{18,26},{24,28},{26,30},{28,20... | collective-permute-start | bytes 3244040 | tf_op jit(solution)/shard_map/ppermute | solution.py:226
  85.9 26.9 %collective-permute-start.13 = (bf16[128,4224]{1,0:T(8,128)(2,1)}, bf16[128,4224]{1,0:T(8,128)(2,1)}, u32[]{:S(2)}, u32[]{:S(2)}) collective-permute-start(bf16[128,4224]{1,0:T(8,128)(2,1)} %collective-permute-done.4.refs_1_.refs_5_.refs_9_), channel_id=1, source_target_pairs={{0,2},{2,0},{4,6},{6,4},{8,10},{10,8},{12,14},{14,12},{16,18},{18,... | collective-permute-start | bytes 3244040 | tf_op jit(solution)/shard_map/ppermute | solution.py:220
  86.1 17.9 %collective-permute-start.15 = (bf16[256,2048]{1,0:T(8,128)(2,1)}, bf16[256,2048]{1,0:T(8,128)(2,1)}, u32[]{:S(2)}, u32[]{:S(2)}) collective-permute-start(bf16[256,2048]{1,0:T(8,128)(2,1)} %get-tuple-element.127), channel_id=1, source_target_pairs={{0,2},{2,0},{4,6},{6,4},{8,10},{10,8},{12,14},{14,12},{16,18},{18,... | collective-permute-start | bytes 3145736 | tf_op jit(solution)/shard_map/ppermute | solution.py:236
  104.0 36.2 %collective-permute-start.11 = (bf16[128,4224]{1,0:T(8,128)(2,1)}, bf16[128,4224]{1,0:T(8,128)(2,1)}, u32[]{:S(2)}, u32[]{:S(2)}) collective-permute-start(bf16[128,4224]{1,0:T(8,128)(2,1)} %collective-permute-done.4.refs_1_.refs_5_.refs_9_), channel_id=1, source_target_pairs={{0,4},{2,6},{8,0},{10,2},{16,8},{18,10},{24,16},{26,18},{28,24},{3... | collective-permute-start | bytes 3244040 | tf_op jit(solution)/shard_map/ppermute | solution.py:227
  106.5 33.8 %collective-permute-start.16 = (bf16[256,2048]{1,0:T(8,128)(2,1)S(1)}, bf16[256,2048]{1,0:T(8,128)(2,1)S(1)}, u32[]{:S(2)}, u32[]{:S(2)}) collective-permute-start(bf16[256,2048]{1,0:T(8,128)(2,1)S(1)} %add_convert_fusion.7), channel_id=1, source_target_pairs={{0,1},{1,0},{2,3},{3,2},{4,5},{5,4},{6,7},{7,6},{8,9},{9,8},{10,11... | collective-permute-start | bytes 3145736 | tf_op jit(solution)/shard_map/ppermute | solution.py:238
  140.3 23.7 %collective-permute-start.19 = (bf16[128,4224]{1,0:T(8,128)(2,1)}, bf16[128,4224]{1,0:T(8,128)(2,1)}, u32[]{:S(2)}, u32[]{:S(2)}) collective-permute-start(bf16[128,4224]{1,0:T(8,128)(2,1)} %collective-permute-done.10.refs_0_.refs_4_.refs_8_), channel_id=1, source_target_pairs={{0,2},{2,0},{4,6},{6,4},{8,10},{10,8},{12,14},{14,12},{16,18},{18,... | collective-permute-start | bytes 3244040 | tf_op jit(solution)/shard_map/ppermute | solution.py:220
  143.3 51.4 %collective-permute-start.17 = (bf16[128,2048]{1,0:T(8,128)(2,1)}, bf16[128,2048]{1,0:T(8,128)(2,1)}, u32[]{:S(2)}, u32[]{:S(2)}) collective-permute-start(bf16[128,2048]{1,0:T(8,128)(2,1)} %get-tuple-element.200), channel_id=1, source_target_pairs={{0,8},{2,10},{8,16},{10,18},{16,24},{18,26},{24,28},{26,30},{28,20... | collective-permute-start | bytes 1572872 | tf_op jit(solution)/shard_map/ppermute | solution.py:229
  144.9 19.9 %collective-permute-start.20 = (bf16[128,4224]{1,0:T(8,128)(2,1)}, bf16[128,4224]{1,0:T(8,128)(2,1)}, u32[]{:S(2)}, u32[]{:S(2)}) collective-permute-start(bf16[128,4224]{1,0:T(8,128)(2,1)} %collective-permute-done.11.refs_1_.refs_5_.refs_9_), channel_id=1, source_target_pairs={{0,2},{2,0},{4,6},{6,4},{8,10},{10,8},{12,14},{14,12},{16,18},{18,... | collective-permute-start | bytes 3244040 | tf_op jit(solution)/shard_map/ppermute | solution.py:220
  144.9 14.9 %collective-permute-start.21 = (bf16[256,2048]{1,0:T(8,128)(2,1)}, bf16[256,2048]{1,0:T(8,128)(2,1)}, u32[]{:S(2)}, u32[]{:S(2)}) collective-permute-start(bf16[256,2048]{1,0:T(8,128)(2,1)} %get-tuple-element.140), channel_id=1, source_target_pairs={{0,2},{2,0},{4,6},{6,4},{8,10},{10,8},{12,14},{14,12},{16,18},{18,... | collective-permute-start | bytes 3145736 | tf_op jit(solution)/shard_map/ppermute | solution.py:237
  156.6 38.2 %collective-permute-start.18 = (bf16[128,2176]{1,0:T(8,128)(2,1)S(1)}, bf16[128,2176]{1,0:T(8,128)(2,1)S(1)}, u32[]{:S(2)}, u32[]{:S(2)}) collective-permute-start(bf16[128,2176]{1,0:T(8,128)(2,1)S(1)} %slice.193), channel_id=1, source_target_pairs={{0,4},{2,6},{8,0},{10,2},{16,8},{18,10},{24,16},{26,18},{28,24},{3... | collective-permute-start | bytes 1671176 | tf_op jit(solution)/shard_map/ppermute | solution.py:230
  159.9 34.9 %collective-permute-start.23 = (bf16[256,2048]{1,0:T(8,128)(2,1)}, bf16[256,2048]{1,0:T(8,128)(2,1)}, u32[]{:S(2)}, u32[]{:S(2)}) collective-permute-start(bf16[256,2048]{1,0:T(8,128)(2,1)} %add_convert_fusion.5), channel_id=1, source_target_pairs={{0,1},{1,0},{2,3},{3,2},{4,5},{5,4},{6,7},{7,6},{8,9},{9,8},{10,11... | collective-permute-start | bytes 3145736 | tf_op jit(solution)/shard_map/ppermute | solution.py:238
  195.3 30.3 %collective-permute-start.26 = (bf16[256,2048]{1,0:T(8,128)(2,1)}, bf16[256,2048]{1,0:T(8,128)(2,1)}, u32[]{:S(2)}, u32[]{:S(2)}) collective-permute-start(bf16[256,2048]{1,0:T(8,128)(2,1)} %get-tuple-element.156), channel_id=1, source_target_pairs={{0,2},{2,0},{4,6},{6,4},{8,10},{10,8},{12,14},{14,12},{16,18},{18,... | collective-permute-start | bytes 3145736 | tf_op jit(solution)/shard_map/ppermute | solution.py:237
  195.4 26.6 %collective-permute-start.27 = (bf16[256,2048]{1,0:T(8,128)(2,1)}, bf16[256,2048]{1,0:T(8,128)(2,1)}, u32[]{:S(2)}, u32[]{:S(2)}) collective-permute-start(bf16[256,2048]{1,0:T(8,128)(2,1)} %get-tuple-element.158), channel_id=1, source_target_pairs={{0,2},{2,0},{4,6},{6,4},{8,10},{10,8},{12,14},{14,12},{16,18},{18,... | collective-permute-start | bytes 3145736 | tf_op jit(solution)/shard_map/ppermute | solution.py:236
  224.1 25.3 %collective-permute-start.28 = (bf16[256,2048]{1,0:T(8,128)(2,1)S(1)}, bf16[256,2048]{1,0:T(8,128)(2,1)}, u32[]{:S(2)}, u32[]{:S(2)}) collective-permute-start(bf16[256,2048]{1,0:T(8,128)(2,1)S(1)} %add_convert_fusion.2), channel_id=1, source_target_pairs={{0,1},{1,0},{2,3},{3,2},{4,5},{5,4},{6,7},{7,6},{8,9},{9,8},{10,11... | collective-permute-start | bytes 3145736 | tf_op jit(solution)/shard_map/ppermute | solution.py:238
  267.9 17.4 %collective-permute-start.30 = (bf16[128,2048]{1,0:T(8,128)(2,1)}, bf16[128,2048]{1,0:T(8,128)(2,1)S(1)}, u32[]{:S(2)}, u32[]{:S(2)}) collective-permute-start(bf16[128,2048]{1,0:T(8,128)(2,1)} %get-tuple-element.174), channel_id=1, source_target_pairs={{0,2},{2,0},{4,6},{6,4},{8,10},{10,8},{12,14},{14,12},{16,18},{18,... | collective-permute-start | bytes 1572872 | tf_op jit(solution)/shard_map/ppermute | solution.py:249
  268.0 26.4 %collective-permute-start.29 = (bf16[128,2048]{1,0:T(8,128)(2,1)}, bf16[128,2048]{1,0:T(8,128)(2,1)}, u32[]{:S(2)}, u32[]{:S(2)}) collective-permute-start(bf16[128,2048]{1,0:T(8,128)(2,1)} %get-tuple-element.172), channel_id=1, source_target_pairs={{0,2},{2,0},{4,6},{6,4},{8,10},{10,8},{12,14},{14,12},{16,18},{18,... | collective-permute-start | bytes 1572872 | tf_op jit(solution)/shard_map/ppermute | solution.py:250
  268.8 15.1 %collective-permute-start.40 = (f32[2048,8]{0,1:T(8,128)S(1)}, f32[2048,8]{0,1:T(8,128)S(1)}, u32[]{:S(2)}, u32[]{:S(2)}) collective-permute-start(f32[2048,8]{0,1:T(8,128)S(1)} %copy.22), channel_id=1, source_target_pairs={{0,1},{1,0},{2,3},{3,2},{4,5},{5,4},{6,7},{7,6},{8,9},{9,8},{10,11... | collective-permute-start | bytes 196616 | tf_op jit(solution)/shard_map/ppermute | solution.py:276
  270.1 87.1 %collective-permute-start.41 = (bf16[16,48,1152]{2,1,0:T(8,128)(2,1)}, bf16[16,48,1152]{2,1,0:T(8,128)(2,1)}, u32[]{:S(2)}, u32[]{:S(2)}) collective-permute-start(bf16[16,48,1152]{2,1,0:T(8,128)(2,1)} %constant_dynamic-update-slice_fusion.30), channel_id=1, source_target_pairs={{0,16},{2,18},{4,20},{6,22},{8,24},{10,26},{12,28},{14,30},{16,0},... | collective-permute-start | bytes 5308424 | tf_op jit(solution)/shard_map/ppermute | solution.py:282
  301.3 15.0 %collective-permute-start.32 = (bf16[128,1024]{1,0:T(8,128)(2,1)S(1)}, bf16[128,1024]{1,0:T(8,128)(2,1)S(1)}, u32[]{:S(2)}, u32[]{:S(2)}) collective-permute-start(bf16[128,1024]{1,0:T(8,128)(2,1)S(1)} %get-tuple-element.227), channel_id=1, source_target_pairs={{0,8},{2,10},{8,16},{10,18},{16,24},{18,26},{24,28},{26,30},{28,20... | collective-permute-start | bytes 786440 | tf_op jit(solution)/shard_map/ppermute | solution.py:266
  317.4 56.5 %collective-permute-start.33 = (bf16[128,2048]{1,0:T(8,128)(2,1)}, bf16[128,2048]{1,0:T(8,128)(2,1)}, u32[]{:S(2)}, u32[]{:S(2)}) collective-permute-start(bf16[128,2048]{1,0:T(8,128)(2,1)} %get-tuple-element.223), channel_id=1, source_target_pairs={{0,8},{2,10},{8,16},{10,18},{16,24},{18,26},{24,28},{26,30},{28,20... | collective-permute-start | bytes 1572872 | tf_op jit(solution)/shard_map/ppermute | solution.py:271
  357.2 16.7 %collective-permute-start.37 = (bf16[128,2048]{1,0:T(8,128)(2,1)S(1)}, bf16[128,2048]{1,0:T(8,128)(2,1)}, u32[]{:S(2)}, u32[]{:S(2)}) collective-permute-start(bf16[128,2048]{1,0:T(8,128)(2,1)S(1)} %get-tuple-element.224), channel_id=1, source_target_pairs={{0,4},{2,6},{8,0},{10,2},{16,8},{18,10},{24,16},{26,18},{28,24},{3... | collective-permute-start | bytes 1572872 | tf_op jit(solution)/shard_map/ppermute | solution.py:272
  375.5 14.5 %collective-permute-start.34 = (bf16[128,2048]{1,0:T(8,128)(2,1)S(1)}, bf16[128,2048]{1,0:T(8,128)(2,1)S(1)}, u32[]{:S(2)}, u32[]{:S(2)}) collective-permute-start(bf16[128,2048]{1,0:T(8,128)(2,1)S(1)} %get-tuple-element.221), channel_id=1, source_target_pairs={{0,8},{2,10},{8,16},{10,18},{16,24},{18,26},{24,28},{26,30},{28,20... | collective-permute-start | bytes 1572872 | tf_op jit(solution)/shard_map/ppermute | solution.py:271
  (52 other events, 469.4 us)
Sparse Core Ops, SparseCore 0:
  304.2 51.6 reduce-scatter.1
